TPU v7x, 512 devices: a whole 4x4x16 slice. The times are simulated.
512 devices in a mesh: tm: 16 (over z), op: 8 (over x, core), spin: 4 (over y).
Axes of the slice: x: 4, y: 4, z: 16, core: 2. Of those that a mesh axis runs over, the one named last changes fastest.
Arguments:
- pairs: int32 [16, 2], replicated, may hold values from 0 to 15, as said below
- elements: bfloat16 [16, 16, 64, 4096], P('tm', 'op', 'spin'), may hold values from -0.119628906 to 0.119628906
- perambs: bfloat16 [16, 16, 3, 4096], P(None, 'spin'), may hold values from -0.75 to 0.75
Outputs:
- correlator: float32 [16, 16, 16], P('tm')
Inputs may be any that keep to these rules, and one draw needn't show every extreme that they name: Column 0 is a pair's source time and column 1 its sink time, never equal. No time slice is the sink of more than 2 pairs, and some time slice is the sink of exactly 2.
All inputs are finite; a program needn't handle non-finite values.
Results may differ from a plain program's by a relative error of at most 0.007.
Values may be sent and summed in bfloat16 or wider, within the bound.
A program may use at most 64 MiB of HBM per device.

v0:
```python
import jax
import jax.numpy as jnp
from jax import lax
from jax.sharding import PartitionSpec as P

MOST = 2


def apply_modes(source, blocks):
    block_count = blocks.shape[0]
    op_count = source.shape[0]
    width = source.shape[1]
    mats = blocks.reshape(block_count, 3, width, width)
    first_mode = jnp.einsum(
        "bxa,jan->bjxn", mats[:, 0], source, preferred_element_type=jnp.float32
    ).astype(jnp.bfloat16)
    first_five = first_mode.reshape(block_count, op_count, width, width, width)
    second_mode = jnp.einsum(
        "byq,bjxqz->bjxyz", mats[:, 1], first_five, preferred_element_type=jnp.float32
    ).astype(jnp.bfloat16)
    third_mode = jnp.einsum(
        "bzc,bjxyc->jxyz", mats[:, 2], second_mode, preferred_element_type=jnp.float32
    )
    return third_mode.astype(jnp.bfloat16).reshape(op_count, width, width * width)


def body(pairs, elements, perambs):
    ops_local = elements.shape[1]
    quarter = elements.shape[2]
    plane = elements.shape[3]
    times_local = elements.shape[0]
    tm_count = lax.axis_size("tm")
    tm_place = lax.axis_index("tm")
    pair_count = pairs.shape[0]
    source_time = pairs[:, 0]
    sink_time = pairs[:, 1]
    positions = jnp.arange(pair_count, dtype=jnp.int32)
    holder = sink_time // times_local
    earlier = (holder[:, None] == holder[None, :]) & (positions[None, :] < positions[:, None])
    standing = jnp.sum(earlier.astype(jnp.int32), axis=1)
    slot_ids = jnp.arange(MOST, dtype=jnp.int32)
    matched = (holder[None, :] == tm_place) & (standing[None, :] == slot_ids[:, None])
    usable = jnp.any(matched, axis=1)
    chosen = jnp.sum(jnp.where(matched, positions[None, :], 0), axis=1)
    slot_total = chosen.shape[0]
    wanted = jnp.stack([source_time[chosen], sink_time[chosen]], axis=1).reshape(-1)
    gathered = lax.all_gather(elements, "tm", axis=0, tiled=True)
    picked = jnp.take(gathered, wanted, axis=0)
    stacked = picked.reshape(slot_total, 2, ops_local, quarter, plane)
    chosen_blocks = jnp.take(perambs, chosen, axis=0)
    full_rows = lax.all_gather(stacked, "spin", axis=3, tiled=True)
    sink_part = lax.all_to_all(full_rows[:, 1], "op", split_axis=2, concat_axis=1, tiled=True)
    products = jnp.stack(
        [
            apply_modes(full_rows[slot_index, 0], chosen_blocks[slot_index])
            for slot_index in range(slot_total)
        ]
    )
    product_part = lax.all_to_all(products, "op", split_axis=2, concat_axis=1, tiled=True)
    partial_value = jnp.einsum(
        "qixn,qjxn->qij", sink_part, product_part, preferred_element_type=jnp.float32
    )
    selector = ((positions[None, :] == chosen[:, None]) & usable[:, None]).astype(jnp.float32)
    spread_table = jnp.einsum(
        "qp,qij->pij", selector, partial_value, precision=lax.Precision.HIGHEST
    )
    summed = lax.psum(spread_table, ("tm", "op", "spin"))
    rows_local = pair_count // tm_count
    return lax.dynamic_slice_in_dim(summed, tm_place * rows_local, rows_local, 0)


def solution(mesh):
    placed = (P(), P("tm", "op", "spin", None), P(None, "spin", None, None))
    return jax.shard_map(
        body, mesh=mesh, in_specs=placed, out_specs=P("tm", None, None), check_vma=False
    )
```

profile of v0, /device:TPU:1, one launch (start us, length us, event | category | flops | bytes accessed | tf_op | source)
XLA Modules:
  0.0 398.2 jit_solution(4367319339344393983)
XLA Ops:
  6.5 0.7 all-gather.3.cloned.1.call-update
  7.3 0.8 slice_bitcast_fusion.19
  8.3 0.7 broadcast_compare_fusion
  9.1 0.6 gather_fusion.1
  9.7 0.6 gather_fusion
  10.7 74.0 %all-gather.3.cloned.1.call-done = bf16[16,2,16,4096]{3,2,1,0:T(8,128)(2,1)} async-done(((bf16[1,2,16,4096]{3,2,1,0:T(8,128)(2,1)}), bf16[16,2,16,4096]{3,2,1,0:T(8,128)(2,1)}) %all-gather.3.cloned.1.call-update) | async-done | bytes 4194320 | tf_op jit(solution)/shard_map/all_gather | solution.py:47
  84.7 2.8 gather_fusion.2
  87.5 1.1 broadcast_select_fusion
  88.7 0.7 gather_fusion.3
  90.1 60.0 %all-gather.5.cloned.1.call-done = bf16[2,2,2,64,4096]{4,3,2,1,0:T(8,128)(2,1)} async-done(((bf16[2,2,2,16,4096]{4,3,2,1,0:T(8,128)(2,1)}), bf16[2,2,2,64,4096]{4,3,2,1,0:T(8,128)(2,1)}) %all-gather.5.cloned.1.call-update) | async-done | bytes 4194320 | tf_op jit(solution)/shard_map/all_gather | solution.py:51
  150.1 4.4 %fusion.18 = bf16[4,2,64,4096]{3,2,0,1:T(8,128)(2,1)} fusion(bf16[2,2,2,64,4096]{4,3,2,1,0:T(8,128)(2,1)} %all-gather.5.cloned.1.call-done, bf16[4,3,64,64]{3,2,0,1:T(8,128)(2,1)S(1)} %reshape_squeeze.6), kind=kOutput, calls=%fused_computation.16 | convolution fusion | flops 270532608 | bytes 5308416 | tf_op jit(solution)/shard_map/bxa,jan->bjxn/dot_general | solution.py:14
  154.5 12.6 %reshape.76 = bf16[4,2,64,64,64]{4,3,2,0,1:T(8,128)(2,1)} reshape(bf16[4,2,64,4096]{3,2,0,1:T(8,128)(2,1)} %fusion.18) | data formatting | bytes 8388608 | tf_op jit(solution)/shard_map/reshape | solution.py:17
  167.1 8.5 %bitcast_convert_fusion.1 = bf16[2,64,64,64]{3,2,1,0:T(8,128)(2,1)} fusion(bf16[4,2,64,64,64]{4,3,2,0,1:T(8,128)(2,1)} %reshape.76, bf16[4,3,64,64]{3,2,0,1:T(8,128)(2,1)S(1)} %reshape_squeeze.6), kind=kOutput, calls=%fused_computation.19 | convolution fusion | flops 539492352 | bytes 5373952 | tf_op jit(solution)/shard_map/bzc,bjxyc->jxyz/dot_general | solution.py:21
  175.5 3.3 stack_reshape.6
  178.9 2.1 copy.64
  180.9 4.4 %fusion.19 = bf16[4,2,64,4096]{3,2,0,1:T(8,128)(2,1)} fusion(bf16[2,2,2,64,4096]{4,3,2,1,0:T(8,128)(2,1)} %all-gather.5.cloned.1.call-done, bf16[4,3,64,64]{3,2,0,1:T(8,128)(2,1)S(1)} %reshape_squeeze.7), kind=kOutput, calls=%fused_computation.17 | convolution fusion | flops 270532608 | bytes 5308416 | tf_op jit(solution)/shard_map/bxa,jan->bjxn/dot_general | solution.py:14
  185.3 12.6 %reshape.77 = bf16[4,2,64,64,64]{4,3,2,0,1:T(8,128)(2,1)} reshape(bf16[4,2,64,4096]{3,2,0,1:T(8,128)(2,1)} %fusion.19) | data formatting | bytes 8388608 | tf_op jit(solution)/shard_map/reshape | solution.py:17
  197.9 8.5 %bitcast_convert_fusion = bf16[2,64,64,64]{3,2,1,0:T(8,128)(2,1)} fusion(bf16[4,2,64,64,64]{4,3,2,0,1:T(8,128)(2,1)} %reshape.77, bf16[4,3,64,64]{3,2,0,1:T(8,128)(2,1)S(1)} %reshape_squeeze.7), kind=kOutput, calls=%fused_computation.18 | convolution fusion | flops 539492352 | bytes 5373952 | tf_op jit(solution)/shard_map/bzc,bjxyc->jxyz/dot_general | solution.py:21
  206.4 3.3 stack_reshape.7
  209.7 1.1 copy.65
  210.8 5.3 %pad_maximum_fusion = bf16[2,2,64,4096]{3,1,0,2:T(2,128)(2,1)} fusion(bf16[1,2,64,4096]{3,1,0,2:T(2,128)(2,1)S(1)} %copy.65, bf16[1,2,64,4096]{3,1,0,2:T(2,128)(2,1)} %copy.64), kind=kLoop, calls=%fused_computation.21 | loop fusion | flops 1048576 | bytes 4194304 | tf_op jit(solution)/shard_map/stack | solution.py:53
  216.1 5.0 %all-to-all-start.1 = ((bf16[2,2,64,4096]{3,1,0,2:T(2,128)(2,1)}), bf16[2,2,64,4096]{3,1,0,2:T(2,128)(2,1)}, u32[]{:S(2)}, u32[]{:S(2)}) async-start(bf16[2,2,64,4096]{3,1,0,2:T(2,128)(2,1)} %pad_maximum_fusion), calls=%async_computation.1 | async-start | bytes 4194304 | tf_op jit(solution)/shard_map/all_to_all | solution.py:59
  221.0 1.7 slice_bitcast_fusion
  222.8 3.5 copy.57
  226.3 21.2 %all-to-all-done.1 = bf16[2,2,64,4096]{3,1,0,2:T(2,128)(2,1)} async-done(((bf16[2,2,64,4096]{3,1,0,2:T(2,128)(2,1)}), bf16[2,2,64,4096]{3,1,0,2:T(2,128)(2,1)}, u32[]{:S(2)}, u32[]{:S(2)}) %all-to-all-start.1) | async-done | bytes 2097184 | tf_op jit(solution)/shard_map/all_to_all | solution.py:59
  247.5 5.1 %all-to-all-start = ((bf16[2,2,64,4096]{3,1,0,2:T(2,128)(2,1)}), bf16[2,2,64,4096]{3,1,0,2:T(2,128)(2,1)}, u32[]{:S(2)}, u32[]{:S(2)}) async-start(bf16[2,2,64,4096]{3,1,0,2:T(2,128)(2,1)} %copy.57), calls=%async_computation | async-start | bytes 4194304 | tf_op jit(solution)/shard_map/all_to_all | solution.py:52
  252.7 2.9 copy.115
  255.6 1.5 copy.67
  257.1 21.9 %all-to-all-done = bf16[2,2,64,4096]{3,1,0,2:T(2,128)(2,1)} async-done(((bf16[2,2,64,4096]{3,1,0,2:T(2,128)(2,1)}), bf16[2,2,64,4096]{3,1,0,2:T(2,128)(2,1)}, u32[]{:S(2)}, u32[]{:S(2)}) %all-to-all-start) | async-done | bytes 2097184 | tf_op jit(solution)/shard_map/all_to_all | solution.py:52
  279.0 3.1 copy.116
  282.3 4.4 %fusion.31 = f32[2,16,16]{2,1,0:T(8,128)S(1)} fusion(bf16[2,16,8,4096]{3,2,1,0:T(8,128)(2,1)S(1)} %bitcast.127, bf16[2,16,8,4096]{3,2,1,0:T(8,128)(2,1)S(1)} %bitcast.128), kind=kOutput, calls=%fused_computation.27 | convolution fusion | flops 33554432 | bytes 4196352 | tf_op jit(solution)/shard_map/qixn,qjxn->qij/dot_general | solution.py:60
  287.1 103.7 %psum.7 = f32[16,16,16]{2,0,1:T(8,128)S(1)} all-reduce(f32[16,16,16]{2,0,1:T(8,128)S(1)} %fusion.36), channel_id=1, replica_groups=mesh['tm'=16,'op'=8,'spin'=4] {'tm','op','spin'}, use_global_device_ids=true, to_apply=%region_3.4 | all-reduce | flops 4096 | bytes 32768 | tf_op jit(solution)/shard_map/psum | solution.py:67
  (27 shorter events, 2.6 us)
Async XLA Ops:
  6.5 82.1 %copy-start = (bf16[16,4,3,4096]{3,1,2,0:T(4,128)(2,1)S(1)}, bf16[16,4,3,4096]{3,1,2,0:T(4,128)(2,1)}, u32[]{:S(2)}) copy-start(bf16[16,4,3,4096]{3,1,2,0:T(4,128)(2,1)} %param.5) | copy-start | bytes 4718596
  6.5 78.2 %all-gather.3.cloned.1.call-start = ((), (), s32[]{:S(2)}) async-start(), calls=%async_computation.2 | async-start | bytes 4456448 | tf_op jit(solution)/shard_map/all_gather | solution.py:47
  7.3 142.8 %all-gather.5.cloned.1.call-start = ((), (), s32[]{:S(2)}) async-start(), calls=%async_computation.3 | async-start | bytes 5242880 | tf_op jit(solution)/shard_map/all_gather | solution.py:51
  216.1 31.4 %all-to-all-start.1 = ((bf16[2,2,64,4096]{3,1,0,2:T(2,128)(2,1)}), bf16[2,2,64,4096]{3,1,0,2:T(2,128)(2,1)}, u32[]{:S(2)}, u32[]{:S(2)}) async-start(bf16[2,2,64,4096]{3,1,0,2:T(2,128)(2,1)} %pad_maximum_fusion), calls=%async_computation.1 | async-start | bytes 4194304 | tf_op jit(solution)/shard_map/all_to_all | solution.py:59
  247.5 31.6 %all-to-all-start = ((bf16[2,2,64,4096]{3,1,0,2:T(2,128)(2,1)}), bf16[2,2,64,4096]{3,1,0,2:T(2,128)(2,1)}, u32[]{:S(2)}, u32[]{:S(2)}) async-start(bf16[2,2,64,4096]{3,1,0,2:T(2,128)(2,1)} %copy.57), calls=%async_computation | async-start | bytes 4194304 | tf_op jit(solution)/shard_map/all_to_all | solution.py:52
  279.0 3.3 copy-start.1
Sparse Core Ops, SparseCore 0:
  9.4 75.2 all-gather.2
  88.8 61.2 all-gather.4
where the time goes:
time: 399 us; the launch traced here: 398 us
  waiting for transfers between devices  178 us (45%)
  blocking collectives  104 us (26%)
  local copies, waits for them, and re-layouts  54.8 us (14%)
  matrix products  30.5 us (8%)
  between operations  13.5 us (3%)
  starting transfers between devices  10.1 us (3%)
  other arithmetic  7.72 us (2%)
    psum x1, blocking collectives, body(): summed = lax.psum(spread_table, ('tm', 'op', 'spin'))  104 us
    all_gather x1, waiting for transfers between devices, body(): gathered = lax.all_gather(elements, 'tm', axis=0, tiled=True)  74 us
    all_gather x1, waiting for transfers between devices, body(): full_rows = lax.all_gather(stacked, 'spin', axis=3, tiled=True)  60 us
    reshape x2, local copies, waits for them, and re-layouts, apply_modes(): first_five = first_mode.reshape(block_count, op_count, width, width, width)  25.2 us
    all_to_all x1, waiting for transfers between devices, body(): lax.all_to_all(full_rows[:, 1], 'op', split_axis=2, concat_axis=1, tiled=...  21.9 us
    all_to_all x1, waiting for transfers between devices, body(): lax.all_to_all(products, 'op', split_axis=2, concat_axis=1, tiled=True)  21.2 us
    dot_general x2, matrix products, apply_modes(): jnp.einsum('bzc,bjxyc->jxyz', mats[:, 2], second_mode, preferred_element_...  16.9 us
    another operation x4, local copies, waits for them, and re-layouts, body(): jnp.stack([apply_modes(full_rows[slot_index, 0], chosen_blocks[slot_index...  9.78 us
  transfers between devices with their start and end apart: 4, of which 4 were waited for; matrix products, arithmetic and copies ran while one was open for 4% of the time, Pallas kernels for 0%

commit v1 on v0

v1 whole, which is shorter than its diff:
```python
import functools

import jax
import jax.numpy as jnp
from jax import lax
from jax.experimental import pallas as pl
from jax.experimental.pallas import tpu as pltpu
from jax.sharding import PartitionSpec as P

MESH = pl.DeviceIdType.MESH
F32 = jnp.float32
BF16 = jnp.bfloat16
NN = (((1,), (0,)), ((), ()))
NT = (((1,), (1,)), ((), ()))


def dot(a, b, dims=NN, precision=None):
    return lax.dot_general(a, b, dims, precision=precision, preferred_element_type=F32)


def iota(shape, axis):
    return lax.broadcasted_iota(jnp.int32, shape, axis)


def kernel(
    zn, pairs, elements, perambs, out,
    win, pv, s8, n64, qn, q0s, bd, q1r, v, t2, s3, prod, sink, rprod, rsink, part, core_part,
    pv_sem, own_recv, own_send, zr, zs, cr, cs, qr, qs, ar, asend, br, bsend, rr, rs, kr, ks,
):
    z, op, y = lax.axis_index("tm"), lax.axis_index("op"), lax.axis_index("spin")
    x, c = op // 2, lax.rem(op, 2)
    chip = x * 4 + y
    other = op + 1 - 2 * c
    up, down = lax.rem(z + 1, zn), lax.rem(z + zn - 1, zn)

    def remote(src, dst, send, recv, device):
        return pltpu.make_async_remote_copy(
            src_ref=src, dst_ref=dst, send_sem=send, recv_sem=recv, device_id=device, device_id_type=MESH
        )

    take_perambs = pltpu.make_async_copy(perambs, pv, pv_sem)
    take_perambs.start()

    barrier = pltpu.get_barrier_semaphore()

    def greet(i, carry):
        o, s = i // 4, lax.rem(i, 4)

        @pl.when(i != op * 4 + y)
        def _():
            pl.semaphore_signal(barrier, inc=1, device_id=(z, o, s), device_id_type=MESH)

        return carry

    lax.fori_loop(0, 32, greet, 0)
    for place in (up, down):
        pl.semaphore_signal(barrier, inc=1, device_id=(place, op, y), device_id_type=MESH)
    pl.semaphore_wait(barrier, 33)

    for k in range(2):
        target = 2 * c + k

        @pl.when(target == y)
        def _(k=k):
            pltpu.make_async_copy(elements.at[0, k], win.at[0, y], own_recv.at[lax.rem(y, 2)]).start()

        @pl.when(target != y)
        def _(k=k, target=target):
            remote(
                elements.at[0, k], win.at[0, y], own_send.at[k], own_recv.at[lax.rem(y, 2)],
                (z, 2 * x + y // 2, target),
            ).start()

    plus_hops, minus_hops = (zn // 2, zn // 2 - 1), (zn // 2 - 1, zn // 2)

    def to_core(slot, k):
        block = win.at[slot, 2 * c + k]
        return remote(block, block, cs.at[slot, k], cr.at[slot, k], (z, other, y))

    def from_core(slot, k):
        block = win.at[slot, 2 * (1 - c) + k]
        return remote(block, block, cs.at[slot, k], cr.at[slot, k], (z, other, y))

    def along(slot, hop, k, way):
        to_slot = hop if way == 0 else zn - hop
        return remote(
            win.at[slot, 2 * c + k], win.at[to_slot, 2 * c + k], zs.at[way, hop, k], zr.at[way, hop, k],
            ((up, down)[way], op, y),
        )

    def hand_on(hop, k):
        for way in range(2):
            hops = (plus_hops, minus_hops)[way]
            slot = 0 if hop == 0 else (hop if way == 0 else zn - hop)
            if hop <= hops[k]:
                if hop > 0:
                    along(slot, hop, k, way).wait_recv()
                if hop < hops[k]:
                    along(slot, hop + 1, k, way).start()
                if hop > 0 or way == 0:
                    to_core(slot, k).start()

    for k in range(2):
        pltpu.make_async_copy(elements.at[0, k], win.at[0, 2 * c + k], own_recv.at[k]).wait()
        hand_on(0, k)

    pair = z
    lane = iota((32, 128), 1) < 64
    take_perambs.wait()

    def flat(b, carry):
        rows = pv[pair, b].astype(F32)
        for t in range(32):
            s8[t * 8:t * 8 + 3, :] = rows[:, t * 128:(t + 1) * 128]
        for l in range(3):
            q = s8[pl.ds(l, 32, stride=8), :]
            r = pltpu.roll(q, 64, 1)
            n64[pl.ds(0, 32, stride=2), :] = jnp.where(lane, q, r)
            n64[pl.ds(1, 32, stride=2), :] = jnp.where(lane, r, q)
            qn[y, b, l] = n64[...].astype(BF16)
        return carry

    lax.fori_loop(0, 4, flat, 0)
    for d in range(1, 4):
        remote(qn.at[y], qn.at[y], qs.at[d], qr.at[d], (z, op, lax.rem(y + d, 4))).start()
    for k in range(2):
        hand_on(1, k)
    for d in range(1, 4):
        remote(qn.at[y], qn.at[lax.rem(y + 4 - d, 4)], qs.at[d], qr.at[d], (z, op, y)).wait_recv()
    for k in range(2):
        hand_on(2, k)

    bd[...] = jnp.zeros_like(bd)
    low = iota((64, 128), 1) < 64

    def blocks(b, carry):
        bq, bb = b // 4, lax.rem(b, 4)
        q0s[pl.ds(b * 32, 32), :] = qn[bq, bb, 0, pl.ds(32 * c, 32), :]
        q2 = qn[bq, bb, 2]
        none = jnp.zeros_like(q2)
        for k in range(4):
            half = jnp.where(low, q2, none) if k % 2 == 0 else jnp.where(low, none, q2)
            bd[b, k * 64:(k + 1) * 64, (k // 2) * 128:(k // 2 + 1) * 128] = half
        return carry

    lax.fori_loop(0, 16, blocks, 0)
    for k in range(2):
        hand_on(3, k)

    rowq, lanel = iota((128, 128), 0), iota((128, 128), 1)
    for g in range(4):
        for lo in range(2):
            acc = jnp.zeros((64, 128), F32)
            for bb in range(4):
                spot = (rowq < 64) & (lax.rem(rowq, 2) == lo) & (lanel == bb * 32 + rowq // 2)
                acc += dot(qn[g, bb, 1], jnp.where(spot, 1.0, 0.0).astype(BF16))
            q1r[lo * 64:(lo + 1) * 64, g * 128:(g + 1) * 128] = acc.astype(BF16)

    for hop in range(4, zn // 2 + 1):
        for k in range(2):
            hand_on(hop, k)
    for slot in range(zn):
        for k in range(2):
            from_core(slot, k).wait_recv()

    source_at = lax.rem(z + zn - pairs[pair, 0], zn)
    sink_at = lax.rem(z + zn - pairs[pair, 1], zn)

    def cut(i, carry):
        k, part_at = i // 8, lax.rem(i, 8)
        sink[i] = win[sink_at, 2 * c + k, :, pl.ds(pl.multiple_of(part_at * 512, 512), 512)]
        return carry

    lax.fori_loop(0, 16, cut, 0)

    def place(xx, yy):
        return lax.rem(yy, 2) * 8 + 2 * xx + yy // 2

    def spread(data, landed, send, recv):
        def one(d, carry):
            xx, yy = lax.rem(x + d // 4, 4), lax.rem(y + lax.rem(d, 4), 4)
            remote(
                data.at[place(xx, yy)], landed.at[chip], send.at[d], recv.at[chip], (z, 2 * xx + c, yy)
            ).start()
            return carry

        lax.fori_loop(1, 16, one, 0)
        landed[chip] = data[place(x, y)]

    def collect(landed, send, recv):
        def one(d, carry):
            e = lax.rem(chip + d, 16)
            remote(landed.at[e], landed.at[e], send.at[d], recv.at[e], (z, op, y)).wait_recv()
            return carry

        lax.fori_loop(1, 16, one, 0)

    spread(sink, rsink, bsend, br)

    def step_one(n, carry):
        columns = win[source_at, :, :, pl.ds(pl.multiple_of(n * 256, 256), 256)].reshape(64, 256)
        first = dot(q0s[:, :64], columns).astype(BF16)
        v[:, n] = first.reshape(16, 32, 256)
        return carry

    lax.fori_loop(0, 16, step_one, 0)

    def step_two(b, carry):
        second = dot(v[b].reshape(512, 256), bd[b], NT)
        for n in range(16):
            for h in range(2):
                start = pl.multiple_of((b * 32 + n * 2 + h) * 32, 32)
                t2[pl.ds(start, 32), :] = second[n * 32:(n + 1) * 32, h * 128:(h + 1) * 128]
        return carry

    lax.fori_loop(0, 16, step_two, 0)

    def step_three(u, carry):
        left = t2[pl.ds(u, 512, stride=32), :].astype(BF16)
        right = t2[pl.ds(u + 16, 512, stride=32), :].astype(BF16)
        both = dot(q1r[...], jnp.concatenate([left, right], axis=1))
        even = both[:64, :128] + pltpu.roll(both[64:, :128], 64, 1)
        odd = pltpu.roll(both[:64, 128:], 64, 1) + both[64:, 128:]
        s3[pl.ds(pl.multiple_of(u * 64, 64), 64), :] = jnp.where(low, even, odd)
        return carry

    lax.fori_loop(0, 16, step_three, 0)
    lane16 = iota((16, 128), 1) < 64

    def natural(p, carry):
        for w in range(4):
            t = p * 4 + w
            a = s3[pl.ds(2 * t, 16, stride=64), :]
            b = s3[pl.ds(2 * t + 1, 16, stride=64), :]
            prod[p, :, w * 128:(w + 1) * 128] = jnp.where(lane16, a, pltpu.roll(b, 64, 1)).astype(BF16)
            prod[8 + p, :, w * 128:(w + 1) * 128] = jnp.where(lane16, pltpu.roll(a, 64, 1), b).astype(BF16)
        return carry

    lax.fori_loop(0, 8, natural, 0)
    spread(prod, rprod, asend, ar)
    collect(rsink, bsend, br)
    collect(rprod, asend, ar)

    grid = dot(rsink[...].reshape(256, 512), rprod[...].reshape(256, 512), NT)
    r256, l256 = iota((256, 256), 0), iota((256, 256), 1)
    same = jnp.where(lax.rem(r256, 16) == lax.rem(l256, 16), grid, 0.0)
    by_row = jnp.sum(same.reshape(16, 16, 256), axis=1)
    gl, gj = iota((256, 128), 0), iota((256, 128), 1)
    gather = jnp.where(gl // 16 == lax.rem(gj, 16), 1.0, 0.0).astype(F32)
    table = dot(by_row, gather, precision=lax.Precision.HIGHEST)
    ti, tl = iota((16, 128), 0), iota((16, 128), 1)
    mine = jnp.where(tl // 16 == lax.rem(ti, 8), table, 0.0)
    part[chip] = jnp.sum(mine.reshape(2, 8, 128), axis=1)

    def tell(d, carry):
        xx, yy = lax.rem(x + d // 4, 4), lax.rem(y + lax.rem(d, 4), 4)
        remote(part.at[chip], part.at[chip], rs.at[d], rr.at[chip], (z, 2 * xx + c, yy)).start()
        return carry

    lax.fori_loop(1, 16, tell, 0)
    collect(part, rs, rr)
    core_part[c] = jnp.sum(part[...], axis=0)
    swap = remote(core_part.at[c], core_part.at[c], ks, kr, (z, other, y))
    swap.start()
    swap.wait_send()
    remote(core_part.at[1 - c], core_part.at[1 - c], ks, kr, (z, other, y)).wait_recv()
    out[...] = core_part[0] + core_part[1]

    for k in range(2):
        @pl.when(2 * c + k != y)
        def _(k=k):
            remote(elements.at[0, k], win.at[0, y], own_send.at[k], own_recv.at[k], (z, op, y)).wait_send()

        for way in range(2):
            for hop in range(1, (plus_hops, minus_hops)[way][k] + 1):
                along(0, hop, k, way).wait_send()
        for slot in range(zn):
            to_core(slot, k).wait_send()
    for d in range(1, 4):
        remote(qn.at[y], qn.at[y], qs.at[d], qr.at[d], (z, op, y)).wait_send()

    def left(d, carry):
        remote(sink.at[0], rsink.at[0], bsend.at[d], br.at[0], (z, op, y)).wait_send()
        remote(prod.at[0], rprod.at[0], asend.at[d], ar.at[0], (z, op, y)).wait_send()
        remote(part.at[0], part.at[0], rs.at[d], rr.at[0], (z, op, y)).wait_send()
        return carry

    lax.fori_loop(1, 16, left, 0)


def solution(mesh):
    zn = mesh.shape["tm"]

    def body(pairs, elements, perambs):
        dma = pltpu.SemaphoreType.DMA
        result = pl.pallas_call(
            functools.partial(kernel, zn),
            out_shape=jax.ShapeDtypeStruct((2, 128), F32),
            in_specs=[
                pl.BlockSpec(memory_space=pltpu.SMEM),
                pl.BlockSpec(memory_space=pl.ANY),
                pl.BlockSpec(memory_space=pl.ANY),
            ],
            out_specs=pl.BlockSpec(memory_space=pltpu.VMEM),
            scratch_shapes=[
                pltpu.VMEM((zn, 4, 16, 4096), BF16),
                pltpu.VMEM((16, 4, 3, 4096), BF16),
                pltpu.VMEM((256, 128), F32),
                pltpu.VMEM((64, 128), F32),
                pltpu.VMEM((4, 4, 3, 64, 128), BF16),
                pltpu.VMEM((512, 128), BF16),
                pltpu.VMEM((16, 256, 256), BF16),
                pltpu.VMEM((128, 512), BF16),
                pltpu.VMEM((16, 16, 32, 256), BF16),
                pltpu.VMEM((16384, 128), F32),
                pltpu.VMEM((1024, 128), F32),
                pltpu.VMEM((16, 16, 512), BF16),
                pltpu.VMEM((16, 16, 512), BF16),
                pltpu.VMEM((16, 16, 512), BF16),
                pltpu.VMEM((16, 16, 512), BF16),
                pltpu.VMEM((16, 2, 128), F32),
                pltpu.VMEM((2, 2, 128), F32),
                dma, dma((2,)), dma((2,)),
                dma((2, zn, 2)), dma((2, zn, 2)), dma((zn, 2)), dma((zn, 2)),
                dma((4,)), dma((4,)),
                dma((16,)), dma((16,)), dma((16,)), dma((16,)), dma((16,)), dma((16,)),
                dma, dma,
            ],
            compiler_params=pltpu.CompilerParams(
                collective_id=0, has_side_effects=True, vmem_limit_bytes=56 * 1024 * 1024
            ),
        )(pairs, elements, perambs)
        return result.reshape(1, 16, 16)

    placed = (P(), P("tm", "op", "spin", None), P(None, "spin", None, None))
    return jax.shard_map(
        body, mesh=mesh, in_specs=placed, out_specs=P("tm", None, None), check_vma=False
    )
```

time: 399 us -> 109 us (0.27)
  waiting for transfers between devices: 178 us -> 0 us
  blocking collectives: 104 us -> 0 us
  Pallas kernels: 0 us -> 101 us
  local copies, waits for them, and re-layouts: 54.8 us -> 7.54 us
  matrix products: 30.5 us -> 0 us
  between operations: 13.5 us -> 0.01 us
  starting transfers between devices: 10.1 us -> 0 us
  other arithmetic: 7.72 us -> 0 us
    all_gather x2 -> x0, waiting for transfers between devices: 134 us -> none  [the longest x1 74 us: body(): gathered = lax.all_gather(elements, 'tm', axis=0, tiled=True)]
    psum x1 -> x0, blocking collectives: 104 us -> none  [body(): summed = lax.psum(spread_table, ('tm', 'op', 'spin'))]
    pallas_call x0 -> x1, Pallas kernels: none -> 101 us  [body(): pl.pallas_call(functools.partial(kernel, zn), out_shape=jax.ShapeDtypeStr...]
    all_to_all x2 -> x0, waiting for transfers between devices: 43.2 us -> none  [the longest x1 21.9 us: body(): lax.all_to_all(full_rows[:, 1], 'op', split_axis=2, concat_axis=1, tiled=...]
    dot_general x6 -> x0, matrix products: 30.5 us -> none  [the longest x2 16.9 us: apply_modes(): jnp.einsum('bzc,bjxyc->jxyz', mats[:, 2], second_mode, preferred_element_...]
    reshape x3 -> x1, local copies, waits for them, and re-layouts: 25.3 us -> 1.36 us  [body(): return result.reshape(1, 16, 16)]
    another operation x7 -> x0, local copies, waits for them, and re-layouts: 10.3 us -> none  [the longest x4 9.78 us: body(): jnp.stack([apply_modes(full_rows[slot_index, 0], chosen_blocks[slot_index...]
    all_to_all x2 -> x0, starting transfers between devices: 10.1 us -> none  [the longest x1 5.12 us: body(): lax.all_to_all(full_rows[:, 1], 'op', split_axis=2, concat_axis=1, tiled=...]
  transfers between devices with their start and end apart: 4 -> 0, of which waited for: 4 -> 0; matrix products, arithmetic and copies ran while one was open for 4% -> 0% of each run, Pallas kernels for 0% -> 0%
where the time goes in v1:
time: 109 us; the launch traced here: 108 us
  Pallas kernels  101 us (93%)
  local copies, waits for them, and re-layouts  7.54 us (7%)
    pallas_call x1, Pallas kernels, body(): pl.pallas_call(functools.partial(kernel, zn), out_shape=jax.ShapeDtypeStr...  101 us
    unnamed x2, local copies, waits for them, and re-layouts  6.17 us

profile of v1, /device:TPU:1, one launch (start us, length us, event | category | flops | bytes accessed | tf_op | source)
XLA Modules:
  0.0 108.4 jit_solution(1650244576325966935)
XLA Ops:
  0.0 1.4 %copy.4.pairs = s32[16,2]{1,0:T(8,128)} copy(s32[16,2]{0,1:T(2,128)} %param.3) | data formatting | bytes 256 | tf_op args[0]
  1.4 4.8 %copy.5.perambs = bf16[16,4,3,4096]{3,2,1,0:T(4,128)(2,1)} copy(bf16[16,4,3,4096]{3,1,2,0:T(4,128)(2,1)} %param.5) | data formatting | bytes 3145728 | tf_op args[2]
  6.2 100.9 %shard_map.37 = f32[2,128]{1,0:T(2,128)} custom-call(s32[16,2]{1,0:T(8,128)} %copy.4.pairs, bf16[1,2,16,4096]{3,2,1,0:T(8,128)(2,1)} %elements.1, bf16[16,4,3,4096]{3,2,1,0:T(4,128)(2,1)} %copy.5.perambs), custom_call_target="tpu_custom_call" | custom-call | tf_op jit(solution)/shard_map/pallas_call | solution.py:296
  107.1 1.4 %reshape.3 = f32[1,16,16]{2,1,0:T(8,128)} reshape(f32[2,128]{1,0:T(2,128)} %shard_map.37) | data formatting | bytes 2048 | tf_op jit(solution)/shard_map/reshape | solution.py:333

commit v2 on v1

--- a/solution.py
+++ b/solution.py
@@ -12,6 +12,7 @@
 BF16 = jnp.bfloat16
 NN = (((1,), (0,)), ((), ()))
 NT = (((1,), (1,)), ((), ()))
+PITCH = 40
 
 
 def dot(a, b, dims=NN, precision=None):
@@ -24,8 +25,8 @@
 
 def kernel(
     zn, pairs, elements, perambs, out,
-    win, pv, s8, n64, qn, q0s, bd, q1r, v, t2, s3, prod, sink, rprod, rsink, part, core_part,
-    pv_sem, own_recv, own_send, zr, zs, cr, cs, qr, qs, ar, asend, br, bsend, rr, rs, kr, ks,
+    win, pv, s8, n64, qn, q0s, bd, q1r, v, t2, prod, sink, rprod, rsink, ks, kp, part, core_part,
+    pv_sem, own_recv, own_send, zr, zs, cr, cs, qr, qs, ar, asend, br, bsend, rr, rs, xr, xs,
 ):
     z, op, y = lax.axis_index("tm"), lax.axis_index("op"), lax.axis_index("spin")
     x, c = op // 2, lax.rem(op, 2)
@@ -108,19 +109,19 @@
     lane = iota((32, 128), 1) < 64
     take_perambs.wait()
 
-    def flat(b, carry):
-        rows = pv[pair, b].astype(F32)
+    def flat(l, carry):
+        rows = pv[pair, l].astype(F32)
         for t in range(32):
-            s8[t * 8:t * 8 + 3, :] = rows[:, t * 128:(t + 1) * 128]
-        for l in range(3):
-            q = s8[pl.ds(l, 32, stride=8), :]
+            s8[t * 8:t * 8 + 4, :] = rows[:, t * 128:(t + 1) * 128]
+        for b in range(4):
+            q = s8[pl.ds(b, 32, stride=8), :]
             r = pltpu.roll(q, 64, 1)
             n64[pl.ds(0, 32, stride=2), :] = jnp.where(lane, q, r)
             n64[pl.ds(1, 32, stride=2), :] = jnp.where(lane, r, q)
             qn[y, b, l] = n64[...].astype(BF16)
         return carry
 
-    lax.fori_loop(0, 4, flat, 0)
+    lax.fori_loop(0, 3, flat, 0)
     for d in range(1, 4):
         remote(qn.at[y], qn.at[y], qs.at[d], qr.at[d], (z, op, lax.rem(y + d, 4))).start()
     for k in range(2):
@@ -163,29 +164,34 @@
         for k in range(2):
             from_core(slot, k).wait_recv()
 
-    source_at = lax.rem(z + zn - pairs[pair, 0], zn)
-    sink_at = lax.rem(z + zn - pairs[pair, 1], zn)
-
-    def cut(i, carry):
-        k, part_at = i // 8, lax.rem(i, 8)
-        sink[i] = win[sink_at, 2 * c + k, :, pl.ds(pl.multiple_of(part_at * 512, 512), 512)]
-        return carry
-
-    lax.fori_loop(0, 16, cut, 0)
-
-    def place(xx, yy):
-        return lax.rem(yy, 2) * 8 + 2 * xx + yy // 2
-
-    def spread(data, landed, send, recv):
+    source_at = lax.rem(z + zn - pairs[0, pair], zn)
+    sink_at = lax.rem(z + zn - pairs[1, pair], zn)
+
+    for k in range(2):
+        def lift(t, carry, k=k):
+            tile = win[sink_at, 2 * c + k, :, pl.ds(pl.multiple_of(t * 128, 128), 128)]
+            t2[pl.ds(pl.multiple_of((k * 32 + t) * 24, 8), 16), :] = tile.astype(F32)
+            return carry
+
+        lax.fori_loop(0, 32, lift, 0, unroll=8)
+
+    def chip_at(d):
+        xx, yy = lax.rem(x + d // 4, 4), lax.rem(y + lax.rem(d, 4), 4)
+        return xx * 4 + yy, (z, 2 * xx + c, yy)
+
+    def cut(u, carry):
+        sink[u] = t2[pl.ds(u, 64, stride=24), :].astype(BF16)
+        return carry
+
+    lax.fori_loop(0, 16, cut, 0, unroll=8)
+
+    def post(data, landed, send, recv):
         def one(d, carry):
-            xx, yy = lax.rem(x + d // 4, 4), lax.rem(y + lax.rem(d, 4), 4)
-            remote(
-                data.at[place(xx, yy)], landed.at[chip], send.at[d], recv.at[chip], (z, 2 * xx + c, yy)
-            ).start()
+            u, device = chip_at(d)
+            remote(data.at[u], landed.at[chip], send.at[d], recv.at[chip], device).start()
             return carry
 
-        lax.fori_loop(1, 16, one, 0)
-        landed[chip] = data[place(x, y)]
+        return one
 
     def collect(landed, send, recv):
         def one(d, carry):
@@ -195,7 +201,8 @@
 
         lax.fori_loop(1, 16, one, 0)
 
-    spread(sink, rsink, bsend, br)
+    lax.fori_loop(1, 16, post(sink, rsink, bsend, br), 0)
+    rsink[chip] = sink[chip]
 
     def step_one(n, carry):
         columns = win[source_at, :, :, pl.ds(pl.multiple_of(n * 256, 256), 256)].reshape(64, 256)
@@ -203,67 +210,66 @@
         v[:, n] = first.reshape(16, 32, 256)
         return carry
 
-    lax.fori_loop(0, 16, step_one, 0)
+    lax.fori_loop(0, 16, step_one, 0, unroll=8)
 
     def step_two(b, carry):
         second = dot(v[b].reshape(512, 256), bd[b], NT)
         for n in range(16):
             for h in range(2):
-                start = pl.multiple_of((b * 32 + n * 2 + h) * 32, 32)
+                start = pl.multiple_of((b * 32 + n * 2 + h) * PITCH, 8)
                 t2[pl.ds(start, 32), :] = second[n * 32:(n + 1) * 32, h * 128:(h + 1) * 128]
         return carry
 
-    lax.fori_loop(0, 16, step_two, 0)
-
-    def step_three(u, carry):
-        left = t2[pl.ds(u, 512, stride=32), :].astype(BF16)
-        right = t2[pl.ds(u + 16, 512, stride=32), :].astype(BF16)
+    lax.fori_loop(0, 16, step_two, 0, unroll=8)
+
+    def step_three(d, carry):
+        u = chip_at(d)[0]
+        left = t2[pl.ds(u, 512, stride=PITCH), :].astype(BF16)
+        right = t2[pl.ds(u + 16, 512, stride=PITCH), :].astype(BF16)
         both = dot(q1r[...], jnp.concatenate([left, right], axis=1))
         even = both[:64, :128] + pltpu.roll(both[64:, :128], 64, 1)
         odd = pltpu.roll(both[:64, 128:], 64, 1) + both[64:, 128:]
-        s3[pl.ds(pl.multiple_of(u * 64, 64), 64), :] = jnp.where(low, even, odd)
-        return carry
-
-    lax.fori_loop(0, 16, step_three, 0)
+        prod[u] = jnp.where(low, even, odd).astype(BF16)
+        return carry
+
+    for start in (1, 5, 9):
+        lax.fori_loop(start, start + 4, step_three, 0, unroll=4)
+        lax.fori_loop(start, start + 4, post(prod, rprod, asend, ar), 0)
+    lax.fori_loop(13, 17, lambda d, carry: step_three(lax.rem(d, 16), carry), 0, unroll=4)
+    lax.fori_loop(13, 16, post(prod, rprod, asend, ar), 0)
+    rprod[chip] = prod[chip]
+
+    collect(rsink, bsend, br)
+    for i in range(16):
+        t2[i * 72:i * 72 + 64, :] = rsink[i].astype(F32)
+    for r in range(64):
+        ks[:, r * 128:(r + 1) * 128] = t2[pl.ds(r, 16, stride=72), :].astype(BF16)
+    collect(rprod, asend, ar)
+    for j in range(16):
+        t2[j * 72:j * 72 + 64, :] = rprod[j].astype(F32)
     lane16 = iota((16, 128), 1) < 64
-
-    def natural(p, carry):
-        for w in range(4):
-            t = p * 4 + w
-            a = s3[pl.ds(2 * t, 16, stride=64), :]
-            b = s3[pl.ds(2 * t + 1, 16, stride=64), :]
-            prod[p, :, w * 128:(w + 1) * 128] = jnp.where(lane16, a, pltpu.roll(b, 64, 1)).astype(BF16)
-            prod[8 + p, :, w * 128:(w + 1) * 128] = jnp.where(lane16, pltpu.roll(a, 64, 1), b).astype(BF16)
-        return carry
-
-    lax.fori_loop(0, 8, natural, 0)
-    spread(prod, rprod, asend, ar)
-    collect(rsink, bsend, br)
-    collect(rprod, asend, ar)
-
-    grid = dot(rsink[...].reshape(256, 512), rprod[...].reshape(256, 512), NT)
-    r256, l256 = iota((256, 256), 0), iota((256, 256), 1)
-    same = jnp.where(lax.rem(r256, 16) == lax.rem(l256, 16), grid, 0.0)
-    by_row = jnp.sum(same.reshape(16, 16, 256), axis=1)
-    gl, gj = iota((256, 128), 0), iota((256, 128), 1)
-    gather = jnp.where(gl // 16 == lax.rem(gj, 16), 1.0, 0.0).astype(F32)
-    table = dot(by_row, gather, precision=lax.Precision.HIGHEST)
-    ti, tl = iota((16, 128), 0), iota((16, 128), 1)
-    mine = jnp.where(tl // 16 == lax.rem(ti, 8), table, 0.0)
+    for t in range(32):
+        a = t2[pl.ds(2 * t, 16, stride=72), :]
+        b = t2[pl.ds(2 * t + 1, 16, stride=72), :]
+        kp[:, t * 128:(t + 1) * 128] = jnp.where(lane16, a, pltpu.roll(b, 64, 1)).astype(BF16)
+        kp[:, (32 + t) * 128:(33 + t) * 128] = jnp.where(lane16, pltpu.roll(a, 64, 1), b).astype(BF16)
+    square = dot(ks[...], kp[...], NT)
+    gl, gj = iota((16, 128), 0), iota((16, 128), 1)
+    table = dot(square, jnp.where(gl == lax.rem(gj, 16), 1.0, 0.0).astype(F32), precision=lax.Precision.HIGHEST)
+    mine = jnp.where(gj // 16 == lax.rem(gl, 8), table, 0.0)
     part[chip] = jnp.sum(mine.reshape(2, 8, 128), axis=1)
 
     def tell(d, carry):
-        xx, yy = lax.rem(x + d // 4, 4), lax.rem(y + lax.rem(d, 4), 4)
-        remote(part.at[chip], part.at[chip], rs.at[d], rr.at[chip], (z, 2 * xx + c, yy)).start()
+        remote(part.at[chip], part.at[chip], rs.at[d], rr.at[chip], chip_at(d)[1]).start()
         return carry
 
     lax.fori_loop(1, 16, tell, 0)
     collect(part, rs, rr)
     core_part[c] = jnp.sum(part[...], axis=0)
-    swap = remote(core_part.at[c], core_part.at[c], ks, kr, (z, other, y))
+    swap = remote(core_part.at[c], core_part.at[c], xs, xr, (z, other, y))
     swap.start()
     swap.wait_send()
-    remote(core_part.at[1 - c], core_part.at[1 - c], ks, kr, (z, other, y)).wait_recv()
+    remote(core_part.at[1 - c], core_part.at[1 - c], xs, xr, (z, other, y)).wait_recv()
     out[...] = core_part[0] + core_part[1]
 
     for k in range(2):
@@ -304,7 +310,7 @@
             out_specs=pl.BlockSpec(memory_space=pltpu.VMEM),
             scratch_shapes=[
                 pltpu.VMEM((zn, 4, 16, 4096), BF16),
-                pltpu.VMEM((16, 4, 3, 4096), BF16),
+                pltpu.VMEM((16, 3, 4, 4096), BF16),
                 pltpu.VMEM((256, 128), F32),
                 pltpu.VMEM((64, 128), F32),
                 pltpu.VMEM((4, 4, 3, 64, 128), BF16),
@@ -312,12 +318,13 @@
                 pltpu.VMEM((16, 256, 256), BF16),
                 pltpu.VMEM((128, 512), BF16),
                 pltpu.VMEM((16, 16, 32, 256), BF16),
-                pltpu.VMEM((16384, 128), F32),
-                pltpu.VMEM((1024, 128), F32),
-                pltpu.VMEM((16, 16, 512), BF16),
-                pltpu.VMEM((16, 16, 512), BF16),
-                pltpu.VMEM((16, 16, 512), BF16),
-                pltpu.VMEM((16, 16, 512), BF16),
+                pltpu.VMEM((512 * PITCH, 128), F32),
+                pltpu.VMEM((16, 64, 128), BF16),
+                pltpu.VMEM((16, 64, 128), BF16),
+                pltpu.VMEM((16, 64, 128), BF16),
+                pltpu.VMEM((16, 64, 128), BF16),
+                pltpu.VMEM((16, 8192), BF16),
+                pltpu.VMEM((16, 8192), BF16),
                 pltpu.VMEM((16, 2, 128), F32),
                 pltpu.VMEM((2, 2, 128), F32),
                 dma, dma((2,)), dma((2,)),
@@ -329,7 +336,7 @@
             compiler_params=pltpu.CompilerParams(
                 collective_id=0, has_side_effects=True, vmem_limit_bytes=56 * 1024 * 1024
             ),
-        )(pairs, elements, perambs)
+        )(pairs.T, elements, perambs.transpose(0, 2, 1, 3))
         return result.reshape(1, 16, 16)
 
     placed = (P(), P("tm", "op", "spin", None), P(None, "spin", None, None))

time: 109 us -> 91 us (0.83)
  Pallas kernels: 101 us -> 89.5 us
  local copies, waits for them, and re-layouts: 7.54 us -> 1.36 us
    pallas_call x1, Pallas kernels: 101 us -> 89.5 us  [body(): pl.pallas_call(functools.partial(kernel, zn), out_shape=jax.ShapeDtypeStr...]
    unnamed x2 -> x0, local copies, waits for them, and re-layouts: 6.17 us -> none
where the time goes in v2:
time: 91 us; the launch traced here: 90.8 us
  Pallas kernels  89.5 us (98%)
  local copies, waits for them, and re-layouts  1.36 us (1%)
    pallas_call x1, Pallas kernels, body(): pl.pallas_call(functools.partial(kernel, zn), out_shape=jax.ShapeDtypeStr...  89.5 us

profile of v2, /device:TPU:1, one launch (start us, length us, event | category | flops | bytes accessed | tf_op | source)
XLA Modules:
  0.0 90.8 jit_solution(684097674731679841)
XLA Ops:
  0.0 89.5 %shard_map.37 = f32[2,128]{1,0:T(2,128)} custom-call(s32[2,16]{1,0:T(2,128)} %bitcast.3, bf16[1,2,16,4096]{3,2,1,0:T(8,128)(2,1)} %elements.1, bf16[16,3,4,4096]{3,2,1,0:T(4,128)(2,1)} %bitcast.2), custom_call_target="tpu_custom_call" | custom-call | tf_op jit(solution)/shard_map/pallas_call | solution.py:302
  89.5 1.4 %reshape.3 = f32[1,16,16]{2,1,0:T(8,128)} reshape(f32[2,128]{1,0:T(2,128)} %shard_map.37) | data formatting | bytes 2048 | tf_op jit(solution)/shard_map/reshape | solution.py:340

commit v3 on v0

v3 whole, which is shorter than its diff:
```python
import functools

import jax
import jax.numpy as jnp
from jax import lax
from jax.experimental import pallas as pl
from jax.experimental.pallas import tpu as pltpu
from jax.sharding import PartitionSpec as P

MESH = pl.DeviceIdType.MESH
F32 = jnp.float32
BF16 = jnp.bfloat16
NN = (((1,), (0,)), ((), ()))
NT = (((1,), (1,)), ((), ()))
PITCH = 40
REACH = 4
TRIES = ((1, 0), (-1, 0), (1, 8), (-1, 8))


def dot(a, b, dims=NN, precision=None):
    return lax.dot_general(a, b, dims, precision=precision, preferred_element_type=F32)


def iota(shape, axis):
    return lax.broadcasted_iota(jnp.int32, shape, axis)


def assign(zn, z, pairs):
    full = (1 << zn) - 1

    def window(centre, reach):
        mask = lax.shift_left(jnp.int32((1 << (2 * reach + 1)) - 1), lax.rem(centre + zn - reach, zn))
        return (mask | lax.shift_right_logical(mask, jnp.int32(zn))) & full

    found, early, late = jnp.int32(0), jnp.int32(-1), jnp.int32(-1)
    for sign, turn in TRIES:
        own = lax.shift_left(jnp.int32(1), lax.rem(sign * z + turn + zn, zn))

        def place(p, state, sign=sign, turn=turn, own=own):
            free_early, free_late, good, mine_early, mine_late = state
            source = lax.rem(sign * pairs[0, p] + turn + zn, zn)
            sink = lax.rem(sign * pairs[1, p] + turn + zn, zn)
            around = window(sink, REACH)
            near = window(source, 2) & around & free_early
            wide = window(source, REACH) & around & free_late
            at_early = near & -near
            at_late = jnp.where(near == 0, wide & -wide, 0)
            return (
                free_early - at_early,
                free_late - at_late,
                jnp.where((at_early | at_late) == 0, 0, good),
                jnp.where(at_early == own, p, mine_early),
                jnp.where(at_late == own, p, mine_late),
            )

        start = (jnp.int32(full), jnp.int32(full), jnp.int32(1), jnp.int32(-1), jnp.int32(-1))
        _, _, good, mine_early, mine_late = lax.fori_loop(0, zn, place, start, unroll=4)
        early = jnp.where(found == 1, early, mine_early)
        late = jnp.where(found == 1, late, mine_late)
        found = jnp.maximum(found, good)
    return found, early, late


def kernel(zn, whole, pairs, elements, perambs, out, *rest):
    if whole:
        flag, rest = None, rest
    else:
        flag, rest = rest[0], rest[1:]
    (near, far, pv, ps, s8, n64, qn, q0s, bd, q1r, v, t2, prod, sink, rprod, rsink, ks, kp, part, zpart, core_part,
     pv_sem, own_recv, own_send, zr, zs, cr, cs, qr, qs, ar, asend, br, bsend, rr, rs, wr, ws, xr, xs) = rest
    slots = 1 if whole else 2
    z, op, y = lax.axis_index("tm"), lax.axis_index("op"), lax.axis_index("spin")
    x, c = op // 2, lax.rem(op, 2)
    chip = x * 4 + y
    other = op + 1 - 2 * c
    up, down = lax.rem(z + 1, zn), lax.rem(z + zn - 1, zn)

    def remote(src, dst, send, recv, device):
        return pltpu.make_async_remote_copy(
            src_ref=src, dst_ref=dst, send_sem=send, recv_sem=recv, device_id=device, device_id_type=MESH
        )

    take_perambs = pltpu.make_async_copy(perambs, pv, pv_sem)
    take_perambs.start()

    barrier = pltpu.get_barrier_semaphore()

    def greet(i, carry):
        o, s = i // 4, lax.rem(i, 4)

        @pl.when(i != op * 4 + y)
        def _():
            pl.semaphore_signal(barrier, inc=1, device_id=(z, o, s), device_id_type=MESH)

        return carry

    lax.fori_loop(0, 32, greet, 0)
    if whole:
        for place in (up, down):
            pl.semaphore_signal(barrier, inc=1, device_id=(place, op, y), device_id_type=MESH)
        pl.semaphore_wait(barrier, 33)
    else:
        def greet_along(d, carry):
            pl.semaphore_signal(barrier, inc=1, device_id=(lax.rem(z + d, zn), op, y), device_id_type=MESH)
            return carry

        lax.fori_loop(1, zn, greet_along, 0)
        pl.semaphore_wait(barrier, 31 + zn - 1)

    odd_y = lax.rem(y, 2)
    for k in range(2):
        j = lax.rem(k + 1 - odd_y, 2)
        target = 2 * c + j

        @pl.when(target != y)
        def _(j=j, target=target):
            remote(
                elements.at[0, j], near.at[0, y], own_send.at[j], own_recv.at[odd_y], (z, 2 * x + y // 2, target)
            ).start()

        @pl.when(target == y)
        def _(j=j):
            pltpu.make_async_copy(elements.at[0, j], near.at[0, y], own_recv.at[odd_y]).start()

    apart = lax.rem(c + y // 2, 2)
    first_piece = lax.rem(odd_y + apart, 2)
    piece = [lax.rem(first_piece + k, 2) for k in range(2)]
    if whole:
        hops = ((zn // 2, zn // 2 - 1), (zn // 2 - 1, zn // 2))
        held = list(range(zn))
    else:
        hops = ((REACH, REACH), (REACH, REACH))
        held = list(range(REACH + 1)) + list(range(zn - REACH, zn))

    def slab(behind):
        if behind <= 2:
            return near.at[behind]
        if behind >= zn - 2:
            return near.at[behind - (zn - 5)]
        if whole or behind <= REACH:
            return far.at[behind - 3]
        return far.at[behind - 3 - (zn - 2 * REACH - 1)]

    def behind_of(way, hop):
        return hop if way == 0 else (zn - hop) % zn

    def to_core(behind, k):
        block = slab(behind).at[2 * c + k]
        return remote(block, block, cs.at[behind, k], cr.at[behind, k], (z, other, y))

    def from_core(behind, k):
        block = slab(behind).at[2 * (1 - c) + k]
        return remote(block, block, cs.at[behind, k], cr.at[behind, k], (z, other, y))

    def along(way, hop, k):
        return remote(
            slab(behind_of(way, hop - 1)).at[2 * c + k], slab(behind_of(way, hop)).at[2 * c + k],
            zs.at[way, hop, k], zr.at[way, hop, k], ((up, down)[way], op, y),
        )

    def hand_on(hop, turn):
        k = piece[turn]
        for way in range(2):
            if hop <= hops[way][turn]:
                if hop > 0:
                    along(way, hop, k).wait_recv()
                if hop < hops[way][turn]:
                    along(way, hop + 1, k).start()
                if hop > 0 or way == 0:
                    to_core(behind_of(way, hop), k).start()

    for turn in range(2):
        k = piece[turn]
        pltpu.make_async_copy(elements.at[0, k], near.at[0, 2 * c + k], own_recv.at[k]).wait()
        hand_on(0, turn)

    if whole:
        work = [z]
    else:
        found, early, late = assign(zn, z, pairs)
        flag[0] = found
        work = [jnp.maximum(early, 0), jnp.maximum(late, 0)]
    take_perambs.wait()
    for n in range(slots):
        ps[n, y] = pv[work[n]]
        for d in range(1, 4):
            remote(ps.at[n, y], ps.at[n, y], qs.at[n, d], qr.at[n, d], (z, op, lax.rem(y + d, 4))).start()
    lane = iota((32, 128), 1) < 64
    low = iota((64, 128), 1) < 64
    bd[...] = jnp.zeros_like(bd)

    def matrices(n):
        for d in range(1, 4):
            remote(
                ps.at[n, y], ps.at[n, lax.rem(y + 4 - d, 4)], qs.at[n, d], qr.at[n, d], (z, op, y)
            ).wait_recv()

        def flat(i, carry):
            g, l = i // 3, lax.rem(i, 3)
            rows = ps[n, g, l].astype(F32)
            for t in range(32):
                s8[t * 8:t * 8 + 4, :] = rows[:, t * 128:(t + 1) * 128]
            for b in range(4):
                q = s8[pl.ds(b, 32, stride=8), :]
                r = pltpu.roll(q, 64, 1)
                n64[pl.ds(b * 64, 32, stride=2), :] = jnp.where(lane, q, r)
                n64[pl.ds(b * 64 + 1, 32, stride=2), :] = jnp.where(lane, r, q)
                qn[g, b, l] = n64[b * 64:(b + 1) * 64, :].astype(BF16)
            return carry

        lax.fori_loop(0, 12, flat, 0)

        def blocks(b, carry):
            g, bb = b // 4, lax.rem(b, 4)
            q0s[pl.ds(b * 32, 32), :] = qn[g, bb, 0, pl.ds(32 * c, 32), :]
            q2 = qn[g, bb, 2]
            none = jnp.zeros_like(q2)
            for k in range(4):
                half = jnp.where(low, q2, none) if k % 2 == 0 else jnp.where(low, none, q2)
                bd[b, k * 64:(k + 1) * 64, (k // 2) * 128:(k // 2 + 1) * 128] = half
            return carry

        lax.fori_loop(0, 16, blocks, 0)
        row, column = iota((128, 128), 0), iota((128, 128), 1)
        for g in range(4):
            for lo in range(2):
                acc = jnp.zeros((64, 128), F32)
                for bb in range(4):
                    spot = (row < 64) & (lax.rem(row, 2) == lo) & (column == bb * 32 + row // 2)
                    acc += dot(qn[g, bb, 1], jnp.where(spot, 1.0, 0.0).astype(BF16))
                q1r[lo * 64:(lo + 1) * 64, g * 128:(g + 1) * 128] = acc.astype(BF16)

    def seek(time):
        behind = lax.rem(z + zn - time, zn)
        is_near = (behind <= 2) | (behind >= zn - 2)
        near_at = jnp.where(is_near, jnp.where(behind <= 2, behind, behind - (zn - 5)), 0)
        if whole:
            far_at = jnp.where(is_near, 0, behind - 3)
        else:
            far_at = jnp.where(behind <= REACH, behind - 3, behind - 3 - (zn - 2 * REACH - 1))
            far_at = jnp.clip(jnp.where(is_near, 0, far_at), 0, 2 * REACH - 5)
        return is_near, near_at, far_at

    def chip_at(d):
        xx, yy = lax.rem(x + d // 4, 4), lax.rem(y + lax.rem(d, 4), 4)
        return xx * 4 + yy, (z, 2 * xx + c, yy)

    def post(data, landed, send, recv):
        def one(d, carry):
            u, device = chip_at(d)
            remote(data.at[u], landed.at[chip], send.at[d], recv.at[chip], device).start()
            return carry

        return one

    def collect(landed, send, recv):
        def one(d, carry):
            e = lax.rem(chip + d, 16)
            remote(landed.at[e], landed.at[e], send.at[d], recv.at[e], (z, op, y)).wait_recv()
            return carry

        lax.fori_loop(1, 16, one, 0)

    def send_sink(n):
        is_near, near_at, far_at = seek(pairs[1, work[n]])
        for k in range(2):
            def lift(t, carry, k=k):
                columns = pl.ds(pl.multiple_of(t * 128, 128), 128)
                tile = jnp.where(is_near, near[near_at, 2 * c + k, :, columns].astype(F32),
                                 far[far_at, 2 * c + k, :, columns].astype(F32))
                t2[pl.ds(pl.multiple_of((k * 32 + t) * 24, 8), 16), :] = tile
                return carry

            lax.fori_loop(0, 32, lift, 0, unroll=8)

        def cut(u, carry):
            sink[n, u] = t2[pl.ds(u, 64, stride=24), :].astype(BF16)
            return carry

        lax.fori_loop(0, 16, cut, 0, unroll=8)
        lax.fori_loop(1, 16, post(sink.at[n], rsink.at[n], bsend.at[n], br.at[n]), 0)
        rsink[n, chip] = sink[n, chip]

    def step_one(n, only_near):
        is_near, near_at, far_at = seek(pairs[0, work[n]])

        def body(t, carry):
            columns = pl.ds(pl.multiple_of(t * 256, 256), 256)
            tile = near[near_at, :, :, columns]
            if not only_near:
                tile = jnp.where(is_near, tile.astype(F32), far[far_at, :, :, columns].astype(F32)).astype(BF16)
            first = dot(q0s[:, :64], tile.reshape(64, 256)).astype(BF16)
            v[:, t] = first.reshape(16, 32, 256)
            return carry

        lax.fori_loop(0, 16, body, 0, unroll=8)

    def step_two():
        def body(b, carry):
            second = dot(v[b].reshape(512, 256), bd[b], NT)
            for n in range(16):
                for h in range(2):
                    start = pl.multiple_of((b * 32 + n * 2 + h) * PITCH, 8)
                    t2[pl.ds(start, 32), :] = second[n * 32:(n + 1) * 32, h * 128:(h + 1) * 128]
            return carry

        lax.fori_loop(0, 16, body, 0, unroll=8)

    def step_three(n):
        def body(d, carry):
            u = chip_at(lax.rem(d, 16))[0]
            left = t2[pl.ds(u, 512, stride=PITCH), :].astype(BF16)
            right = t2[pl.ds(u + 16, 512, stride=PITCH), :].astype(BF16)
            both = dot(q1r[...], jnp.concatenate([left, right], axis=1))
            even = both[:64, :128] + pltpu.roll(both[64:, :128], 64, 1)
            odd = pltpu.roll(both[:64, 128:], 64, 1) + both[64:, 128:]
            prod[n, u] = jnp.where(low, even, odd).astype(BF16)
            return carry

        for start in (1, 5, 9, 13):
            lax.fori_loop(start, start + 4, body, 0, unroll=4)
            send = post(prod.at[n], rprod.at[n], asend.at[n], ar.at[n])
            lax.fori_loop(start, min(start + 4, 16), send, 0)
        rprod[n, chip] = prod[n, chip]

    if whole:
        for hop in range(1, max(hops[0]) + 1):
            for turn in range(2):
                hand_on(hop, turn)
            if hop == 1:
                matrices(0)
        for behind in held:
            for k in range(2):
                from_core(behind, k).wait_recv()
    else:
        for turn in range(2):
            hand_on(1, turn)
        matrices(0)
        for turn in range(2):
            hand_on(2, turn)
        close = [b for b in held if b <= 2 or b >= zn - 2]
        for behind in close:
            for k in range(2):
                from_core(behind, k).wait_recv()
        step_one(0, True)
        hand_on(3, 0)
        step_two()
        hand_on(3, 1)
        step_three(0)
        hand_on(4, 0)
        matrices(1)
        hand_on(4, 1)
        for behind in held:
            if behind not in close:
                for k in range(2):
                    from_core(behind, k).wait_recv()

    last = slots - 1
    for n in reversed(range(slots)):
        send_sink(n)
    step_one(last, False)
    step_two()
    step_three(last)

    lane16 = iota((16, 128), 1) < 64
    wl, wj = iota((16, 128), 0), iota((16, 128), 1)

    def contract(n):
        collect(rsink.at[n], bsend.at[n], br.at[n])
        for i in range(16):
            t2[i * 72:i * 72 + 64, :] = rsink[n, i].astype(F32)
        for r in range(64):
            ks[:, r * 128:(r + 1) * 128] = t2[pl.ds(r, 16, stride=72), :].astype(BF16)
        collect(rprod.at[n], asend.at[n], ar.at[n])
        for j in range(16):
            t2[j * 72:j * 72 + 64, :] = rprod[n, j].astype(F32)
        for t in range(32):
            a = t2[pl.ds(2 * t, 16, stride=72), :]
            b = t2[pl.ds(2 * t + 1, 16, stride=72), :]
            kp[:, t * 128:(t + 1) * 128] = jnp.where(lane16, a, pltpu.roll(b, 64, 1)).astype(BF16)
            kp[:, (32 + t) * 128:(33 + t) * 128] = jnp.where(lane16, pltpu.roll(a, 64, 1), b).astype(BF16)
        square = dot(ks[...], kp[...], NT)
        table = dot(square, jnp.where(wl == lax.rem(wj, 16), 1.0, 0.0).astype(F32), precision=lax.Precision.HIGHEST)
        mine = jnp.where(wj // 16 == lax.rem(wl, 8), table, 0.0)
        return jnp.sum(mine.reshape(2, 8, 128), axis=1)

    tables = [contract(n) for n in range(slots)]
    if whole:
        part[chip] = tables[0]
    else:
        for d in range(zn):
            p = lax.rem(z + d, zn)
            zpart[1, d] = jnp.where(early == p, tables[0], 0.0) + jnp.where(late == p, tables[1], 0.0)
            if d > 0:
                remote(zpart.at[1, d], zpart.at[0, d], ws.at[d], wr.at[d], (p, op, y)).start()
        zpart[0, 0] = zpart[1, 0]
        for d in range(1, zn):
            remote(zpart.at[1, d], zpart.at[0, d], ws.at[d], wr.at[d], (z, op, y)).wait_recv()
        part[chip] = jnp.sum(zpart[0], axis=0)

    def tell(d, carry):
        remote(part.at[chip], part.at[chip], rs.at[d], rr.at[chip], chip_at(d)[1]).start()
        return carry

    lax.fori_loop(1, 16, tell, 0)
    collect(part, rs, rr)
    core_part[c] = jnp.sum(part[...], axis=0)
    swap = remote(core_part.at[c], core_part.at[c], xs, xr, (z, other, y))
    swap.start()
    swap.wait_send()
    remote(core_part.at[1 - c], core_part.at[1 - c], xs, xr, (z, other, y)).wait_recv()
    out[...] = core_part[0] + core_part[1]

    for k in range(2):
        @pl.when(2 * c + k != y)
        def _(k=k):
            remote(elements.at[0, k], near.at[0, y], own_send.at[k], own_recv.at[k], (z, op, y)).wait_send()

        for way in range(2):
            for hop in range(1, hops[way][k] + 1):
                along(way, hop, piece[k]).wait_send()
        for behind in held:
            to_core(behind, k).wait_send()
    for n in range(slots):
        for d in range(1, 4):
            remote(ps.at[n, y], ps.at[n, y], qs.at[n, d], qr.at[n, d], (z, op, y)).wait_send()

        def left(d, carry, n=n):
            remote(sink.at[n, 0], rsink.at[n, 0], bsend.at[n, d], br.at[n, 0], (z, op, y)).wait_send()
            remote(prod.at[n, 0], rprod.at[n, 0], asend.at[n, d], ar.at[n, 0], (z, op, y)).wait_send()
            return carry

        lax.fori_loop(1, 16, left, 0)

    def left_tables(d, carry):
        remote(part.at[0], part.at[0], rs.at[d], rr.at[0], (z, op, y)).wait_send()
        return carry

    lax.fori_loop(1, 16, left_tables, 0)
    if not whole:
        for d in range(1, zn):
            remote(zpart.at[1, d], zpart.at[0, d], ws.at[d], wr.at[d], (z, op, y)).wait_send()


def call(zn, whole, pairs, elements, perambs):
    dma = pltpu.SemaphoreType.DMA
    slots = 1 if whole else 2
    far = zn - 5 if whole else 2 * REACH - 4
    out_shape = [jax.ShapeDtypeStruct((2, 128), F32)]
    out_specs = [pl.BlockSpec(memory_space=pltpu.VMEM)]
    if not whole:
        out_shape.append(jax.ShapeDtypeStruct((1,), jnp.int32))
        out_specs.append(pl.BlockSpec(memory_space=pltpu.SMEM))
    return pl.pallas_call(
        functools.partial(kernel, zn, whole),
        out_shape=out_shape,
        in_specs=[
            pl.BlockSpec(memory_space=pltpu.SMEM),
            pl.BlockSpec(memory_space=pl.ANY),
            pl.BlockSpec(memory_space=pl.ANY),
        ],
        out_specs=out_specs,
        scratch_shapes=[
            pltpu.VMEM((5, 4, 16, 4096), BF16),
            pltpu.VMEM((far, 4, 16, 4096), BF16),
            pltpu.VMEM((16, 3, 4, 4096), BF16),
            pltpu.VMEM((slots, 4, 3, 4, 4096), BF16),
            pltpu.VMEM((256, 128), F32),
            pltpu.VMEM((256, 128), F32),
            pltpu.VMEM((4, 4, 3, 64, 128), BF16),
            pltpu.VMEM((512, 128), BF16),
            pltpu.VMEM((16, 256, 256), BF16),
            pltpu.VMEM((128, 512), BF16),
            pltpu.VMEM((16, 16, 32, 256), BF16),
            pltpu.VMEM((512 * PITCH, 128), F32),
            pltpu.VMEM((slots, 16, 64, 128), BF16),
            pltpu.VMEM((slots, 16, 64, 128), BF16),
            pltpu.VMEM((slots, 16, 64, 128), BF16),
            pltpu.VMEM((slots, 16, 64, 128), BF16),
            pltpu.VMEM((16, 8192), BF16),
            pltpu.VMEM((16, 8192), BF16),
            pltpu.VMEM((16, 2, 128), F32),
            pltpu.VMEM((2, zn, 2, 128), F32),
            pltpu.VMEM((2, 2, 128), F32),
            dma, dma((2,)), dma((2,)),
            dma((2, zn, 2)), dma((2, zn, 2)), dma((zn, 2)), dma((zn, 2)),
            dma((slots, 4)), dma((slots, 4)),
            dma((slots, 16)), dma((slots, 16)), dma((slots, 16)), dma((slots, 16)), dma((16,)), dma((16,)),
            dma((zn,)), dma((zn,)), dma, dma,
        ],
        compiler_params=pltpu.CompilerParams(
            collective_id=1 if whole else 0, has_side_effects=True, vmem_limit_bytes=56 * 1024 * 1024
        ),
    )(pairs, elements, perambs)


def solution(mesh):
    zn = mesh.shape["tm"]

    def body(pairs, elements, perambs):
        given = (pairs.T, elements, perambs.transpose(0, 2, 1, 3))
        table = call(zn, True, *given)[0]
        return table.reshape(1, 16, 16)

    placed = (P(), P("tm", "op", "spin", None), P(None, "spin", None, None))
    return jax.shard_map(
        body, mesh=mesh, in_specs=placed, out_specs=P("tm", None, None), check_vma=False
    )
```

time: 399 us -> 90.4 us (0.23)
  waiting for transfers between devices: 178 us -> 0 us
  blocking collectives: 104 us -> 0 us
  Pallas kernels: 0 us -> 88.9 us
  local copies, waits for them, and re-layouts: 54.8 us -> 1.36 us
  matrix products: 30.5 us -> 0 us
  between operations: 13.5 us -> 0.01 us
  starting transfers between devices: 10.1 us -> 0 us
  other arithmetic: 7.72 us -> 0 us
    all_gather x2 -> x0, waiting for transfers between devices: 134 us -> none  [the longest x1 74 us: body(): gathered = lax.all_gather(elements, 'tm', axis=0, tiled=True)]
    psum x1 -> x0, blocking collectives: 104 us -> none  [body(): summed = lax.psum(spread_table, ('tm', 'op', 'spin'))]
    pallas_call x0 -> x1, Pallas kernels: none -> 88.9 us  [call(): pl.pallas_call(functools.partial(kernel, zn, whole), out_shape=out_shape,...]
    all_to_all x2 -> x0, waiting for transfers between devices: 43.2 us -> none  [the longest x1 21.9 us: body(): lax.all_to_all(full_rows[:, 1], 'op', split_axis=2, concat_axis=1, tiled=...]
    dot_general x6 -> x0, matrix products: 30.5 us -> none  [the longest x2 16.9 us: apply_modes(): jnp.einsum('bzc,bjxyc->jxyz', mats[:, 2], second_mode, preferred_element_...]
    reshape x3 -> x1, local copies, waits for them, and re-layouts: 25.3 us -> 1.36 us  [body(): return table.reshape(1, 16, 16)]
    another operation x7 -> x0, local copies, waits for them, and re-layouts: 10.3 us -> none  [the longest x4 9.78 us: body(): jnp.stack([apply_modes(full_rows[slot_index, 0], chosen_blocks[slot_index...]
    all_to_all x2 -> x0, starting transfers between devices: 10.1 us -> none  [the longest x1 5.12 us: body(): lax.all_to_all(full_rows[:, 1], 'op', split_axis=2, concat_axis=1, tiled=...]
  transfers between devices with their start and end apart: 4 -> 0, of which waited for: 4 -> 0; matrix products, arithmetic and copies ran while one was open for 4% -> 0% of each run, Pallas kernels for 0% -> 0%
where the time goes in v3:
time: 90.4 us; the launch traced here: 90.3 us
  Pallas kernels  88.9 us (98%)
  local copies, waits for them, and re-layouts  1.36 us (2%)
    pallas_call x1, Pallas kernels, call(): pl.pallas_call(functools.partial(kernel, zn, whole), out_shape=out_shape,...  88.9 us

profile of v3, /device:TPU:1, one launch (start us, length us, event | category | flops | bytes accessed | tf_op | source)
XLA Modules:
  0.0 90.3 jit_solution(884539303955487806)
XLA Ops:
  0.0 88.9 %shard_map.37 = f32[2,128]{1,0:T(2,128)} custom-call(s32[2,16]{1,0:T(2,128)} %bitcast.3, bf16[1,2,16,4096]{3,2,1,0:T(8,128)(2,1)} %elements.1, bf16[16,3,4,4096]{3,2,1,0:T(4,128)(2,1)} %bitcast.2), custom_call_target="tpu_custom_call" | custom-call | tf_op jit(solution)/shard_map/pallas_call | solution.py:454
  88.9 1.4 %reshape.3 = f32[1,16,16]{2,1,0:T(8,128)} reshape(f32[2,128]{1,0:T(2,128)} %shard_map.37) | data formatting | bytes 2048 | tf_op jit(solution)/shard_map/reshape | solution.py:503

commit v4 on v3

--- a/solution.py
+++ b/solution.py
@@ -66,9 +66,11 @@
         flag, rest = None, rest
     else:
         flag, rest = rest[0], rest[1:]
-    (near, far, pv, ps, s8, n64, qn, q0s, bd, q1r, v, t2, prod, sink, rprod, rsink, ks, kp, part, zpart, core_part,
+    slots = 1 if whole else 2
+    own, rest = rest[:5 * slots], rest[5 * slots:]
+    ps, prod, sink, rprod, rsink = (own[i * slots:(i + 1) * slots] for i in range(5))
+    (near, far, pv, s8, n64, qn, q0s, bd, q1r, v, t2, ks, kp, part, zout, zin, core_part,
      pv_sem, own_recv, own_send, zr, zs, cr, cs, qr, qs, ar, asend, br, bsend, rr, rs, wr, ws, xr, xs) = rest
-    slots = 1 if whole else 2
     z, op, y = lax.axis_index("tm"), lax.axis_index("op"), lax.axis_index("spin")
     x, c = op // 2, lax.rem(op, 2)
     chip = x * 4 + y
@@ -182,9 +184,9 @@
         work = [jnp.maximum(early, 0), jnp.maximum(late, 0)]
     take_perambs.wait()
     for n in range(slots):
-        ps[n, y] = pv[work[n]]
+        ps[n][y] = pv[work[n]]
         for d in range(1, 4):
-            remote(ps.at[n, y], ps.at[n, y], qs.at[n, d], qr.at[n, d], (z, op, lax.rem(y + d, 4))).start()
+            remote(ps[n].at[y], ps[n].at[y], qs.at[n, d], qr.at[n, d], (z, op, lax.rem(y + d, 4))).start()
     lane = iota((32, 128), 1) < 64
     low = iota((64, 128), 1) < 64
     bd[...] = jnp.zeros_like(bd)
@@ -192,12 +194,11 @@
     def matrices(n):
         for d in range(1, 4):
             remote(
-                ps.at[n, y], ps.at[n, lax.rem(y + 4 - d, 4)], qs.at[n, d], qr.at[n, d], (z, op, y)
+                ps[n].at[y], ps[n].at[lax.rem(y + 4 - d, 4)], qs.at[n, d], qr.at[n, d], (z, op, y)
             ).wait_recv()
 
-        def flat(i, carry):
-            g, l = i // 3, lax.rem(i, 3)
-            rows = ps[n, g, l].astype(F32)
+        def flat(l, carry, g):
+            rows = ps[n][g, l].astype(F32)
             for t in range(32):
                 s8[t * 8:t * 8 + 4, :] = rows[:, t * 128:(t + 1) * 128]
             for b in range(4):
@@ -208,7 +209,8 @@
                 qn[g, b, l] = n64[b * 64:(b + 1) * 64, :].astype(BF16)
             return carry
 
-        lax.fori_loop(0, 12, flat, 0)
+        for g in range(4):
+            lax.fori_loop(0, 3, functools.partial(flat, g=g), 0)
 
         def blocks(b, carry):
             g, bb = b // 4, lax.rem(b, 4)
@@ -274,12 +276,12 @@
             lax.fori_loop(0, 32, lift, 0, unroll=8)
 
         def cut(u, carry):
-            sink[n, u] = t2[pl.ds(u, 64, stride=24), :].astype(BF16)
+            sink[n][u] = t2[pl.ds(u, 64, stride=24), :].astype(BF16)
             return carry
 
         lax.fori_loop(0, 16, cut, 0, unroll=8)
-        lax.fori_loop(1, 16, post(sink.at[n], rsink.at[n], bsend.at[n], br.at[n]), 0)
-        rsink[n, chip] = sink[n, chip]
+        lax.fori_loop(1, 16, post(sink[n], rsink[n], bsend.at[n], br.at[n]), 0)
+        rsink[n][chip] = sink[n][chip]
 
     def step_one(n, only_near):
         is_near, near_at, far_at = seek(pairs[0, work[n]])
@@ -314,14 +316,14 @@
             both = dot(q1r[...], jnp.concatenate([left, right], axis=1))
             even = both[:64, :128] + pltpu.roll(both[64:, :128], 64, 1)
             odd = pltpu.roll(both[:64, 128:], 64, 1) + both[64:, 128:]
-            prod[n, u] = jnp.where(low, even, odd).astype(BF16)
+            prod[n][u] = jnp.where(low, even, odd).astype(BF16)
             return carry
 
         for start in (1, 5, 9, 13):
             lax.fori_loop(start, start + 4, body, 0, unroll=4)
-            send = post(prod.at[n], rprod.at[n], asend.at[n], ar.at[n])
+            send = post(prod[n], rprod[n], asend.at[n], ar.at[n])
             lax.fori_loop(start, min(start + 4, 16), send, 0)
-        rprod[n, chip] = prod[n, chip]
+        rprod[n][chip] = prod[n][chip]
 
     if whole:
         for hop in range(1, max(hops[0]) + 1):
@@ -366,14 +368,14 @@
     wl, wj = iota((16, 128), 0), iota((16, 128), 1)
 
     def contract(n):
-        collect(rsink.at[n], bsend.at[n], br.at[n])
+        collect(rsink[n], bsend.at[n], br.at[n])
         for i in range(16):
-            t2[i * 72:i * 72 + 64, :] = rsink[n, i].astype(F32)
+            t2[i * 72:i * 72 + 64, :] = rsink[n][i].astype(F32)
         for r in range(64):
             ks[:, r * 128:(r + 1) * 128] = t2[pl.ds(r, 16, stride=72), :].astype(BF16)
-        collect(rprod.at[n], asend.at[n], ar.at[n])
+        collect(rprod[n], asend.at[n], ar.at[n])
         for j in range(16):
-            t2[j * 72:j * 72 + 64, :] = rprod[n, j].astype(F32)
+            t2[j * 72:j * 72 + 64, :] = rprod[n][j].astype(F32)
         for t in range(32):
             a = t2[pl.ds(2 * t, 16, stride=72), :]
             b = t2[pl.ds(2 * t + 1, 16, stride=72), :]
@@ -390,13 +392,13 @@
     else:
         for d in range(zn):
             p = lax.rem(z + d, zn)
-            zpart[1, d] = jnp.where(early == p, tables[0], 0.0) + jnp.where(late == p, tables[1], 0.0)
+            zout[d] = jnp.where(early == p, tables[0], 0.0) + jnp.where(late == p, tables[1], 0.0)
             if d > 0:
-                remote(zpart.at[1, d], zpart.at[0, d], ws.at[d], wr.at[d], (p, op, y)).start()
-        zpart[0, 0] = zpart[1, 0]
+                remote(zout.at[d], zin.at[d], ws.at[d], wr.at[d], (p, op, y)).start()
+        zin[0] = zout[0]
         for d in range(1, zn):
-            remote(zpart.at[1, d], zpart.at[0, d], ws.at[d], wr.at[d], (z, op, y)).wait_recv()
-        part[chip] = jnp.sum(zpart[0], axis=0)
+            remote(zout.at[d], zin.at[d], ws.at[d], wr.at[d], (z, op, y)).wait_recv()
+        part[chip] = jnp.sum(zin[...], axis=0)
 
     def tell(d, carry):
         remote(part.at[chip], part.at[chip], rs.at[d], rr.at[chip], chip_at(d)[1]).start()
@@ -423,11 +425,11 @@
             to_core(behind, k).wait_send()
     for n in range(slots):
         for d in range(1, 4):
-            remote(ps.at[n, y], ps.at[n, y], qs.at[n, d], qr.at[n, d], (z, op, y)).wait_send()
+            remote(ps[n].at[y], ps[n].at[y], qs.at[n, d], qr.at[n, d], (z, op, y)).wait_send()
 
         def left(d, carry, n=n):
-            remote(sink.at[n, 0], rsink.at[n, 0], bsend.at[n, d], br.at[n, 0], (z, op, y)).wait_send()
-            remote(prod.at[n, 0], rprod.at[n, 0], asend.at[n, d], ar.at[n, 0], (z, op, y)).wait_send()
+            remote(sink[n].at[0], rsink[n].at[0], bsend.at[n, d], br.at[n, 0], (z, op, y)).wait_send()
+            remote(prod[n].at[0], rprod[n].at[0], asend.at[n, d], ar.at[n, 0], (z, op, y)).wait_send()
             return carry
 
         lax.fori_loop(1, 16, left, 0)
@@ -439,7 +441,7 @@
     lax.fori_loop(1, 16, left_tables, 0)
     if not whole:
         for d in range(1, zn):
-            remote(zpart.at[1, d], zpart.at[0, d], ws.at[d], wr.at[d], (z, op, y)).wait_send()
+            remote(zout.at[d], zin.at[d], ws.at[d], wr.at[d], (z, op, y)).wait_send()
 
 
 def call(zn, whole, pairs, elements, perambs):
@@ -461,10 +463,11 @@
         ],
         out_specs=out_specs,
         scratch_shapes=[
+            *[pltpu.VMEM((4, 3, 4, 4096), BF16)] * slots,
+            *[pltpu.VMEM((16, 64, 128), BF16)] * (4 * slots),
             pltpu.VMEM((5, 4, 16, 4096), BF16),
             pltpu.VMEM((far, 4, 16, 4096), BF16),
             pltpu.VMEM((16, 3, 4, 4096), BF16),
-            pltpu.VMEM((slots, 4, 3, 4, 4096), BF16),
             pltpu.VMEM((256, 128), F32),
             pltpu.VMEM((256, 128), F32),
             pltpu.VMEM((4, 4, 3, 64, 128), BF16),
@@ -473,14 +476,11 @@
             pltpu.VMEM((128, 512), BF16),
             pltpu.VMEM((16, 16, 32, 256), BF16),
             pltpu.VMEM((512 * PITCH, 128), F32),
-            pltpu.VMEM((slots, 16, 64, 128), BF16),
-            pltpu.VMEM((slots, 16, 64, 128), BF16),
-            pltpu.VMEM((slots, 16, 64, 128), BF16),
-            pltpu.VMEM((slots, 16, 64, 128), BF16),
             pltpu.VMEM((16, 8192), BF16),
             pltpu.VMEM((16, 8192), BF16),
             pltpu.VMEM((16, 2, 128), F32),
-            pltpu.VMEM((2, zn, 2, 128), F32),
+            pltpu.VMEM((zn, 2, 128), F32),
+            pltpu.VMEM((zn, 2, 128), F32),
             pltpu.VMEM((2, 2, 128), F32),
             dma, dma((2,)), dma((2,)),
             dma((2, zn, 2)), dma((2, zn, 2)), dma((zn, 2)), dma((zn, 2)),
@@ -499,7 +499,8 @@
 
     def body(pairs, elements, perambs):
         given = (pairs.T, elements, perambs.transpose(0, 2, 1, 3))
-        table = call(zn, True, *given)[0]
+        table, found = call(zn, False, *given)
+        table = lax.cond(found[0] == 1, lambda: table, lambda: call(zn, True, *given)[0])
         return table.reshape(1, 16, 16)
 
     placed = (P(), P("tm", "op", "spin", None), P(None, "spin", None, None))

time: 90.4 us -> 80.8 us (0.89)
  Pallas kernels: 88.9 us -> 79.2 us
    pallas_call x1, Pallas kernels: 88.9 us -> 79.2 us  [call(): pl.pallas_call(functools.partial(kernel, zn, whole), out_shape=out_shape,...]
    reshape x1, local copies, waits for them, and re-layouts: 1.36 us -> 0.08 us  [body(): return table.reshape(1, 16, 16)]
where the time goes in v4:
time: 80.8 us; the launch traced here: 80.7 us
  Pallas kernels  79.2 us (98%)
    pallas_call x1, Pallas kernels, call(): pl.pallas_call(functools.partial(kernel, zn, whole), out_shape=out_shape,...  79.2 us

profile of v4, /device:TPU:1, one launch (start us, length us, event | category | flops | bytes accessed | tf_op | source)
XLA Modules:
  0.0 80.7 jit_solution(11270407286397822065)
XLA Ops:
  0.0 0.0 copy-start.1
  0.0 0.0 copy-start
  0.0 0.0 copy-start.3
  0.0 79.2 %shard_map.39 = (f32[2,128]{1,0:T(2,128)S(1)}, s32[1]{0:T(128)}) custom-call(s32[2,16]{1,0:T(2,128)} %bitcast.5, bf16[1,2,16,4096]{3,2,1,0:T(8,128)(2,1)} %elements.1, bf16[16,3,4,4096]{3,2,1,0:T(4,128)(2,1)} %bitcast.3), custom_call_target="tpu_custom_call" | custom-call | tf_op jit(solution)/shard_map/pallas_call | solution.py:456
  79.9 0.0 copy-done.1
  79.9 0.0 copy-done
  80.0 0.0 copy-done.3
  80.0 0.1 conditional.1
  80.0 0.1 reshape.10
  80.1 0.0 copy-start.2
  80.1 0.6 copy-done.2
Async XLA Ops:
  0.0 79.9 %copy-start.1 = (bf16[1,2,16,4096]{3,2,1,0:T(8,128)(2,1)S(1)}, bf16[1,2,16,4096]{3,2,1,0:T(8,128)(2,1)}, u32[]{:S(2)}) copy-start(bf16[1,2,16,4096]{3,2,1,0:T(8,128)(2,1)} %elements.1) | copy-start | bytes 786436
  0.0 79.9 %copy-start = (bf16[16,4,3,4096]{3,1,2,0:T(4,128)(2,1)S(1)}, bf16[16,4,3,4096]{3,1,2,0:T(4,128)(2,1)}, u32[]{:S(2)}) copy-start(bf16[16,4,3,4096]{3,1,2,0:T(4,128)(2,1)} %param.7) | copy-start | bytes 4718596
  0.0 80.0 %copy-start.3 = (s32[16,2]{0,1:T(2,128)S(1)}, s32[16,2]{0,1:T(2,128)}, u32[]{:S(2)}) copy-start(s32[16,2]{0,1:T(2,128)} %param.5) | copy-start | bytes 388
  80.1 0.6 copy-start.2

commit v5 on v4

--- a/solution.py
+++ b/solution.py
@@ -69,8 +69,8 @@
     slots = 1 if whole else 2
     own, rest = rest[:5 * slots], rest[5 * slots:]
     ps, prod, sink, rprod, rsink = (own[i * slots:(i + 1) * slots] for i in range(5))
-    (near, far, pv, s8, n64, qn, q0s, bd, q1r, v, t2, ks, kp, part, zout, zin, core_part,
-     pv_sem, own_recv, own_send, zr, zs, cr, cs, qr, qs, ar, asend, br, bsend, rr, rs, wr, ws, xr, xs) = rest
+    (near, far, pv, s8, n64, qn, q0s, bd, q1r, v, t2, ks, kp, part, zout, zin,
+     pv_sem, own_recv, own_send, zr, zs, cr, cs, qr, qs, ar, asend, br, bsend, rr, rs, wr, ws, token) = rest
     z, op, y = lax.axis_index("tm"), lax.axis_index("op"), lax.axis_index("spin")
     x, c = op // 2, lax.rem(op, 2)
     chip = x * 4 + y
@@ -97,17 +97,9 @@
         return carry
 
     lax.fori_loop(0, 32, greet, 0)
-    if whole:
-        for place in (up, down):
-            pl.semaphore_signal(barrier, inc=1, device_id=(place, op, y), device_id_type=MESH)
-        pl.semaphore_wait(barrier, 33)
-    else:
-        def greet_along(d, carry):
-            pl.semaphore_signal(barrier, inc=1, device_id=(lax.rem(z + d, zn), op, y), device_id_type=MESH)
-            return carry
-
-        lax.fori_loop(1, zn, greet_along, 0)
-        pl.semaphore_wait(barrier, 31 + zn - 1)
+    for place in (up, down):
+        pl.semaphore_signal(barrier, inc=1, device_id=(place, op, y), device_id_type=MESH)
+    pl.semaphore_wait(barrier, 33)
 
     odd_y = lax.rem(y, 2)
     for k in range(2):
@@ -183,10 +175,13 @@
         flag[0] = found
         work = [jnp.maximum(early, 0), jnp.maximum(late, 0)]
     take_perambs.wait()
-    for n in range(slots):
+
+    def send_perambs(n):
         ps[n][y] = pv[work[n]]
         for d in range(1, 4):
             remote(ps[n].at[y], ps[n].at[y], qs.at[n, d], qr.at[n, d], (z, op, lax.rem(y + d, 4))).start()
+
+    send_perambs(0)
     lane = iota((32, 128), 1) < 64
     low = iota((64, 128), 1) < 64
     bd[...] = jnp.zeros_like(bd)
@@ -340,6 +335,7 @@
         matrices(0)
         for turn in range(2):
             hand_on(2, turn)
+        send_perambs(1)
         close = [b for b in held if b <= 2 or b >= zn - 2]
         for behind in close:
             for k in range(2):
@@ -352,6 +348,10 @@
         hand_on(4, 0)
         matrices(1)
         hand_on(4, 1)
+        for away in (REACH, zn - REACH):
+            pl.semaphore_signal(
+                token, inc=1, device_id=(lax.rem(z + away, zn), op, y), device_id_type=MESH
+            )
         for behind in held:
             if behind not in close:
                 for k in range(2):
@@ -387,9 +387,11 @@
         return jnp.sum(mine.reshape(2, 8, 128), axis=1)
 
     tables = [contract(n) for n in range(slots)]
+    place = op * 4 + y
     if whole:
-        part[chip] = tables[0]
+        part[place] = tables[0]
     else:
+        pl.semaphore_wait(token, 2)
         for d in range(zn):
             p = lax.rem(z + d, zn)
             zout[d] = jnp.where(early == p, tables[0], 0.0) + jnp.where(late == p, tables[1], 0.0)
@@ -398,20 +400,21 @@
         zin[0] = zout[0]
         for d in range(1, zn):
             remote(zout.at[d], zin.at[d], ws.at[d], wr.at[d], (z, op, y)).wait_recv()
-        part[chip] = jnp.sum(zin[...], axis=0)
-
-    def tell(d, carry):
-        remote(part.at[chip], part.at[chip], rs.at[d], rr.at[chip], chip_at(d)[1]).start()
-        return carry
-
-    lax.fori_loop(1, 16, tell, 0)
-    collect(part, rs, rr)
-    core_part[c] = jnp.sum(part[...], axis=0)
-    swap = remote(core_part.at[c], core_part.at[c], xs, xr, (z, other, y))
-    swap.start()
-    swap.wait_send()
-    remote(core_part.at[1 - c], core_part.at[1 - c], xs, xr, (z, other, y)).wait_recv()
-    out[...] = core_part[0] + core_part[1]
+        part[place] = jnp.sum(zin[...], axis=0)
+
+    def tell(d):
+        o, s = lax.rem(op + d // 4, 8), lax.rem(y + d % 4, 4)
+        return remote(part.at[place], part.at[place], rs.at[d], rr.at[d], (z, o, s))
+
+    def told(d):
+        o, s = lax.rem(op + 8 - d // 4, 8), lax.rem(y + 4 - d % 4, 4)
+        return remote(part.at[place], part.at[o * 4 + s], rs.at[d], rr.at[d], (z, op, y))
+
+    for d in range(1, 32):
+        tell(d).start()
+    for d in range(1, 32):
+        told(d).wait_recv()
+    out[...] = jnp.sum(part[...], axis=0)
 
     for k in range(2):
         @pl.when(2 * c + k != y)
@@ -434,11 +437,8 @@
 
         lax.fori_loop(1, 16, left, 0)
 
-    def left_tables(d, carry):
-        remote(part.at[0], part.at[0], rs.at[d], rr.at[0], (z, op, y)).wait_send()
-        return carry
-
-    lax.fori_loop(1, 16, left_tables, 0)
+    for d in range(1, 32):
+        tell(d).wait_send()
     if not whole:
         for d in range(1, zn):
             remote(zout.at[d], zin.at[d], ws.at[d], wr.at[d], (z, op, y)).wait_send()
@@ -478,15 +478,14 @@
             pltpu.VMEM((512 * PITCH, 128), F32),
             pltpu.VMEM((16, 8192), BF16),
             pltpu.VMEM((16, 8192), BF16),
-            pltpu.VMEM((16, 2, 128), F32),
+            pltpu.VMEM((32, 2, 128), F32),
             pltpu.VMEM((zn, 2, 128), F32),
             pltpu.VMEM((zn, 2, 128), F32),
-            pltpu.VMEM((2, 2, 128), F32),
             dma, dma((2,)), dma((2,)),
             dma((2, zn, 2)), dma((2, zn, 2)), dma((zn, 2)), dma((zn, 2)),
             dma((slots, 4)), dma((slots, 4)),
-            dma((slots, 16)), dma((slots, 16)), dma((slots, 16)), dma((slots, 16)), dma((16,)), dma((16,)),
-            dma((zn,)), dma((zn,)), dma, dma,
+            dma((slots, 16)), dma((slots, 16)), dma((slots, 16)), dma((slots, 16)), dma((32,)), dma((32,)),
+            dma((zn,)), dma((zn,)), pltpu.SemaphoreType.REGULAR,
         ],
         compiler_params=pltpu.CompilerParams(
             collective_id=1 if whole else 0, has_side_effects=True, vmem_limit_bytes=56 * 1024 * 1024

time: 80.8 us -> 78.6 us (0.973)
  Pallas kernels: 79.2 us -> 77.1 us
    pallas_call x1, Pallas kernels: 79.2 us -> 77.1 us  [call(): pl.pallas_call(functools.partial(kernel, zn, whole), out_shape=out_shape,...]
where the time goes in v5:
time: 78.6 us; the launch traced here: 78.5 us
  Pallas kernels  77.1 us (98%)
    pallas_call x1, Pallas kernels, call(): pl.pallas_call(functools.partial(kernel, zn, whole), out_shape=out_shape,...  77.1 us

profile of v5, /device:TPU:1, one launch (start us, length us, event | category | flops | bytes accessed | tf_op | source)
XLA Modules:
  0.0 78.5 jit_solution(10123818332989977322)
XLA Ops:
  0.0 0.0 copy-start.1
  0.0 0.0 copy-start
  0.0 0.0 copy-start.3
  0.0 77.1 %shard_map.39 = (f32[2,128]{1,0:T(2,128)S(1)}, s32[1]{0:T(128)}) custom-call(s32[2,16]{1,0:T(2,128)} %bitcast.5, bf16[1,2,16,4096]{3,2,1,0:T(8,128)(2,1)} %elements.1, bf16[16,3,4,4096]{3,2,1,0:T(4,128)(2,1)} %bitcast.3), custom_call_target="tpu_custom_call" | custom-call | tf_op jit(solution)/shard_map/pallas_call | solution.py:456
  77.8 0.0 copy-done.1
  77.8 0.0 copy-done
  77.8 0.0 copy-done.3
  77.8 0.1 conditional.1
  77.8 0.1 reshape.10
  77.9 0.0 copy-start.2
  77.9 0.6 copy-done.2
Async XLA Ops:
  0.0 77.8 %copy-start.1 = (bf16[1,2,16,4096]{3,2,1,0:T(8,128)(2,1)S(1)}, bf16[1,2,16,4096]{3,2,1,0:T(8,128)(2,1)}, u32[]{:S(2)}) copy-start(bf16[1,2,16,4096]{3,2,1,0:T(8,128)(2,1)} %elements.1) | copy-start | bytes 786436
  0.0 77.8 %copy-start = (bf16[16,4,3,4096]{3,1,2,0:T(4,128)(2,1)S(1)}, bf16[16,4,3,4096]{3,1,2,0:T(4,128)(2,1)}, u32[]{:S(2)}) copy-start(bf16[16,4,3,4096]{3,1,2,0:T(4,128)(2,1)} %param.7) | copy-start | bytes 4718596
  0.0 77.8 %copy-start.3 = (s32[16,2]{0,1:T(2,128)S(1)}, s32[16,2]{0,1:T(2,128)}, u32[]{:S(2)}) copy-start(s32[16,2]{0,1:T(2,128)} %param.5) | copy-start | bytes 388
  77.9 0.6 copy-start.2

commit v6 on v5

--- a/solution.py
+++ b/solution.py
@@ -14,6 +14,8 @@
 NT = (((1,), (1,)), ((), ()))
 PITCH = 40
 REACH = 4
+FAR_CHIPS = sorted(range(1, 16), key=lambda d: -(min(d // 4, 4 - d // 4) + min(d % 4, 4 - d % 4)))
+FAR_PLACES = sorted(range(1, 32), key=lambda d: -(min(d // 4, 8 - d // 4) / 2 + min(d % 4, 4 - d % 4)))
 TRIES = ((1, 0), (-1, 0), (1, 8), (-1, 8))
 
 
@@ -239,7 +241,7 @@
         return is_near, near_at, far_at
 
     def chip_at(d):
-        xx, yy = lax.rem(x + d // 4, 4), lax.rem(y + lax.rem(d, 4), 4)
+        xx, yy = lax.rem(x + d // 4, 4), lax.rem(y + d % 4, 4)
         return xx * 4 + yy, (z, 2 * xx + c, yy)
 
     def post(data, landed, send, recv):
@@ -275,7 +277,9 @@
             return carry
 
         lax.fori_loop(0, 16, cut, 0, unroll=8)
-        lax.fori_loop(1, 16, post(sink[n], rsink[n], bsend.at[n], br.at[n]), 0)
+        send = post(sink[n], rsink[n], bsend.at[n], br.at[n])
+        for d in FAR_CHIPS:
+            send(d, 0)
         rsink[n][chip] = sink[n][chip]
 
     def step_one(n, only_near):
@@ -290,7 +294,7 @@
             v[:, t] = first.reshape(16, 32, 256)
             return carry
 
-        lax.fori_loop(0, 16, body, 0, unroll=8)
+        lax.fori_loop(0, 16, body, 0, unroll=16)
 
     def step_two():
         def body(b, carry):
@@ -301,11 +305,11 @@
                     t2[pl.ds(start, 32), :] = second[n * 32:(n + 1) * 32, h * 128:(h + 1) * 128]
             return carry
 
-        lax.fori_loop(0, 16, body, 0, unroll=8)
+        lax.fori_loop(0, 16, body, 0, unroll=16)
 
     def step_three(n):
         def body(d, carry):
-            u = chip_at(lax.rem(d, 16))[0]
+            u = chip_at(d)[0]
             left = t2[pl.ds(u, 512, stride=PITCH), :].astype(BF16)
             right = t2[pl.ds(u + 16, 512, stride=PITCH), :].astype(BF16)
             both = dot(q1r[...], jnp.concatenate([left, right], axis=1))
@@ -314,10 +318,14 @@
             prod[n][u] = jnp.where(low, even, odd).astype(BF16)
             return carry
 
-        for start in (1, 5, 9, 13):
-            lax.fori_loop(start, start + 4, body, 0, unroll=4)
-            send = post(prod[n], rprod[n], asend.at[n], ar.at[n])
-            lax.fori_loop(start, min(start + 4, 16), send, 0)
+        order = FAR_CHIPS + [0]
+        send = post(prod[n], rprod[n], asend.at[n], ar.at[n])
+        for start in (0, 4, 8, 12):
+            for d in order[start:start + 4]:
+                body(d, 0)
+            for d in order[start:start + 4]:
+                if d:
+                    send(d, 0)
         rprod[n][chip] = prod[n][chip]
 
     if whole:
@@ -392,7 +400,7 @@
         part[place] = tables[0]
     else:
         pl.semaphore_wait(token, 2)
-        for d in range(zn):
+        for d in sorted(range(zn), key=lambda d: -min(d, zn - d)):
             p = lax.rem(z + d, zn)
             zout[d] = jnp.where(early == p, tables[0], 0.0) + jnp.where(late == p, tables[1], 0.0)
             if d > 0:
@@ -410,7 +418,7 @@
         o, s = lax.rem(op + 8 - d // 4, 8), lax.rem(y + 4 - d % 4, 4)
         return remote(part.at[place], part.at[o * 4 + s], rs.at[d], rr.at[d], (z, op, y))
 
-    for d in range(1, 32):
+    for d in FAR_PLACES:
         tell(d).start()
     for d in range(1, 32):
         told(d).wait_recv()

time: 78.6 us -> 77.1 us (0.981)
  Pallas kernels: 77.1 us -> 75.5 us
    pallas_call x1, Pallas kernels: 77.1 us -> 75.5 us  [call(): pl.pallas_call(functools.partial(kernel, zn, whole), out_shape=out_shape,...]
where the time goes in v6:
time: 77.1 us; the launch traced here: 76.9 us
  Pallas kernels  75.5 us (98%)
    pallas_call x1, Pallas kernels, call(): pl.pallas_call(functools.partial(kernel, zn, whole), out_shape=out_shape,...  75.5 us

profile of v6, /device:TPU:1, one launch (start us, length us, event | category | flops | bytes accessed | tf_op | source)
XLA Modules:
  0.0 76.9 jit_solution(10167723134540624614)
XLA Ops:
  0.0 0.0 copy-start.1
  0.0 0.0 copy-start
  0.0 0.0 copy-start.3
  0.0 75.5 %shard_map.39 = (f32[2,128]{1,0:T(2,128)S(1)}, s32[1]{0:T(128)}) custom-call(s32[2,16]{1,0:T(2,128)} %bitcast.5, bf16[1,2,16,4096]{3,2,1,0:T(8,128)(2,1)} %elements.1, bf16[16,3,4,4096]{3,2,1,0:T(4,128)(2,1)} %bitcast.3), custom_call_target="tpu_custom_call" | custom-call | tf_op jit(solution)/shard_map/pallas_call | solution.py:464
  76.2 0.0 copy-done.1
  76.2 0.0 copy-done
  76.2 0.0 copy-done.3
  76.2 0.1 conditional.1
  76.3 0.1 reshape.10
  76.3 0.0 copy-start.2
  76.3 0.6 copy-done.2
Async XLA Ops:
  0.0 76.2 %copy-start.1 = (bf16[1,2,16,4096]{3,2,1,0:T(8,128)(2,1)S(1)}, bf16[1,2,16,4096]{3,2,1,0:T(8,128)(2,1)}, u32[]{:S(2)}) copy-start(bf16[1,2,16,4096]{3,2,1,0:T(8,128)(2,1)} %elements.1) | copy-start | bytes 786436
  0.0 76.2 %copy-start = (bf16[16,4,3,4096]{3,1,2,0:T(4,128)(2,1)S(1)}, bf16[16,4,3,4096]{3,1,2,0:T(4,128)(2,1)}, u32[]{:S(2)}) copy-start(bf16[16,4,3,4096]{3,1,2,0:T(4,128)(2,1)} %param.7) | copy-start | bytes 4718596
  0.0 76.2 %copy-start.3 = (s32[16,2]{0,1:T(2,128)S(1)}, s32[16,2]{0,1:T(2,128)}, u32[]{:S(2)}) copy-start(s32[16,2]{0,1:T(2,128)} %param.5) | copy-start | bytes 388
  76.3 0.6 copy-start.2

commit v7 on v6

--- a/solution.py
+++ b/solution.py
@@ -476,14 +476,14 @@
             pltpu.VMEM((5, 4, 16, 4096), BF16),
             pltpu.VMEM((far, 4, 16, 4096), BF16),
             pltpu.VMEM((16, 3, 4, 4096), BF16),
-            pltpu.VMEM((256, 128), F32),
-            pltpu.VMEM((256, 128), F32),
+            pltpu.VMEM((272, 128), F32),
+            pltpu.VMEM((272, 128), F32),
             pltpu.VMEM((4, 4, 3, 64, 128), BF16),
             pltpu.VMEM((512, 128), BF16),
             pltpu.VMEM((16, 256, 256), BF16),
             pltpu.VMEM((128, 512), BF16),
             pltpu.VMEM((16, 16, 32, 256), BF16),
-            pltpu.VMEM((512 * PITCH, 128), F32),
+            pltpu.VMEM((512 * PITCH + 64, 128), F32),
             pltpu.VMEM((16, 8192), BF16),
             pltpu.VMEM((16, 8192), BF16),
             pltpu.VMEM((32, 2, 128), F32),

time: 77.1 us -> 77.1 us (level)
  no operation moved by 1% of the time
where the time goes in v7:
time: 77.1 us; the launch traced here: 76.9 us
  Pallas kernels  75.5 us (98%)
    pallas_call x1, Pallas kernels, call(): pl.pallas_call(functools.partial(kernel, zn, whole), out_shape=out_shape,...  75.5 us

profile of v7, /device:TPU:1, one launch (start us, length us, event | category | flops | bytes accessed | tf_op | source)
XLA Modules:
  0.0 76.9 jit_solution(3690986738063271546)
XLA Ops:
  0.0 0.0 copy-start.1
  0.0 0.0 copy-start
  0.0 0.0 copy-start.3
  0.0 75.5 %shard_map.39 = (f32[2,128]{1,0:T(2,128)S(1)}, s32[1]{0:T(128)}) custom-call(s32[2,16]{1,0:T(2,128)} %bitcast.5, bf16[1,2,16,4096]{3,2,1,0:T(8,128)(2,1)} %elements.1, bf16[16,3,4,4096]{3,2,1,0:T(4,128)(2,1)} %bitcast.3), custom_call_target="tpu_custom_call" | custom-call | tf_op jit(solution)/shard_map/pallas_call | solution.py:464
  76.2 0.0 copy-done.1
  76.2 0.0 copy-done
  76.2 0.0 copy-done.3
  76.2 0.1 conditional.1
  76.3 0.1 reshape.10
  76.3 0.0 copy-start.2
  76.3 0.6 copy-done.2
Async XLA Ops:
  0.0 76.2 %copy-start.1 = (bf16[1,2,16,4096]{3,2,1,0:T(8,128)(2,1)S(1)}, bf16[1,2,16,4096]{3,2,1,0:T(8,128)(2,1)}, u32[]{:S(2)}) copy-start(bf16[1,2,16,4096]{3,2,1,0:T(8,128)(2,1)} %elements.1) | copy-start | bytes 786436
  0.0 76.2 %copy-start = (bf16[16,4,3,4096]{3,1,2,0:T(4,128)(2,1)S(1)}, bf16[16,4,3,4096]{3,1,2,0:T(4,128)(2,1)}, u32[]{:S(2)}) copy-start(bf16[16,4,3,4096]{3,1,2,0:T(4,128)(2,1)} %param.7) | copy-start | bytes 4718596
  0.0 76.2 %copy-start.3 = (s32[16,2]{0,1:T(2,128)S(1)}, s32[16,2]{0,1:T(2,128)}, u32[]{:S(2)}) copy-start(s32[16,2]{0,1:T(2,128)} %param.5) | copy-start | bytes 388
  76.3 0.6 copy-start.2
